TPU v7x, 512 devices: a whole 4x8x8 slice. The times are simulated.
512 devices in a mesh: dp: 32 (over z_lo, y, core), tensor: 16 (over z_hi, x).
Axes of the slice: x: 4, y: 8, z: 8 (z_hi: 4, z_lo: 2; z = z_hi * 2 + z_lo), core: 2. Of those that a mesh axis runs over, the one named last changes fastest.
Arguments:
- inputs: bfloat16 [32, 128, 5120], P('dp', None, 'tensor'), may hold values from -6 to 6
- w_qkv: bfloat16 [3, 5120, 4096], P(None, 'dp', 'tensor'), may hold values from -0.078125 to 0.078125
- w_gates: bfloat16 [2, 5120, 32], P(None, None, 'tensor'), may hold values from -0.078125 to 0.078125
- conv_weight: float32 [3, 4, 4096], P(None, None, 'tensor'), may hold values from -3 to 3
- decay_rate: float32 [32], P('tensor'), may hold values from 0.002 to 0.1
- gate_bias: float32 [32], P('tensor'), may hold values from -2 to 2
- norm_gain: float32 [128], replicated, may hold values from 0.5 to 1.5
- w_out: bfloat16 [4096, 5120], P('tensor', 'dp'), may hold values from -0.09375 to 0.09375
- grad_out: bfloat16 [32, 128, 5120], P('dp', None, 'tensor'), may hold values from -0.1796875 to 0.1796875
Outputs:
- output: bfloat16 [32, 128, 5120], P('dp', None, 'tensor')
- grad_in: bfloat16 [32, 128, 5120], P('dp', None, 'tensor')
- grad_gates: float32 [2, 5120, 32], P(None, None, 'tensor')
- grad_conv: float32 [3, 4, 4096], P(None, None, 'tensor')
- grad_rate: float32 [32], P('tensor')
- grad_bias: float32 [32], P('tensor')
- grad_gain: float32 [128], replicated
All inputs are finite; a program needn't handle non-finite values.
Results may differ from a plain program's by a relative error of at most 0.019.
Values may be sent and summed in bfloat16 or wider, within the bound.
A program may use at most 64 MiB of HBM per device.

v0:
```python
import math

import jax
import jax.numpy as jnp
from jax import lax
from jax.sharding import PartitionSpec as P

BLOCK = 64


HI = lax.Precision.HIGHEST


def head_scan(queries, key_rows, value_rows, decays, strength):
    block_count = queries.shape[0] // BLOCK

    def to_blocks(array):
        return array.reshape((block_count, BLOCK) + array.shape[1:])

    position = jnp.arange(BLOCK)
    strict = position[:, None] > position[None, :]
    within = position[:, None] >= position[None, :]

    def advance(carried, block_items):
        query_part, key_part, value_part, decay_part, write_part = block_items
        cumulative = jnp.cumsum(decay_part)
        spread = jnp.where(within, cumulative[:, None] - cumulative[None, :], 0.0)
        fading = jnp.where(within, jnp.exp(spread), 0.0)
        key_dots = jnp.dot(key_part, key_part.T, precision=HI)
        system = jnp.eye(BLOCK, dtype=queries.dtype) + write_part[:, None] * jnp.where(
            strict, fading * key_dots, 0.0
        )
        growth = jnp.exp(cumulative)[:, None]
        target = write_part[:, None] * (
            value_part - growth * jnp.dot(key_part, carried.T, precision=HI)
        )
        update_rows = jax.scipy.linalg.solve_triangular(
            system, target, lower=True, unit_diagonal=True
        )
        scores = fading * jnp.dot(query_part, key_part.T, precision=HI)
        result = growth * jnp.dot(query_part, carried.T, precision=HI) + jnp.dot(
            scores, update_rows, precision=HI
        )
        remain = jnp.exp(cumulative[-1] - cumulative)[:, None]
        carried = jnp.exp(cumulative[-1]) * carried + jnp.dot(
            (update_rows * remain).T, key_part, precision=HI
        )
        return (carried, result)

    initial = jnp.zeros((value_rows.shape[1], key_rows.shape[1]), queries.dtype)
    _, results = lax.scan(
        advance,
        initial,
        (
            to_blocks(queries),
            to_blocks(key_rows),
            to_blocks(value_rows),
            to_blocks(decays),
            to_blocks(strength),
        ),
    )
    return results.reshape(queries.shape[0], value_rows.shape[1])


def layer_core(projected, logits, conv_weight, decay_rate, gate_bias, norm_gain):
    length = projected.shape[1]
    head_count = decay_rate.shape[0]
    tap_count = conv_weight.shape[1]
    padded = jnp.pad(projected, ((0, 0), (tap_count - 1, 0), (0, 0)))
    convolved = conv_weight[:, 0][:, None, :] * padded[:, 0:length]
    for offset in range(1, tap_count):
        convolved = (
            convolved + conv_weight[:, offset][:, None, :] * padded[:, offset : offset + length]
        )
    active = jax.nn.silu(convolved).reshape(3, length, head_count, -1)
    head_width = active.shape[-1]
    queries = (
        active[0]
        / jnp.sqrt(jnp.sum(active[0] * active[0], -1, keepdims=True) + 1e-06)
        / math.sqrt(head_width)
    )
    key_rows = active[1] / jnp.sqrt(jnp.sum(active[1] * active[1], -1, keepdims=True) + 1e-06)
    value_rows = active[2]
    strength = jax.nn.sigmoid(logits[1])
    decays = -decay_rate * jax.nn.softplus(logits[0] + gate_bias)
    heads_out = jax.vmap(head_scan, in_axes=(1, 1, 1, 1, 1), out_axes=1)(
        queries, key_rows, value_rows, decays, strength
    )
    row_scale = jnp.sqrt(jnp.mean(heads_out * heads_out, -1, keepdims=True) + 1e-05)
    normed = heads_out / row_scale * norm_gain
    return normed.reshape(length, -1)


def on_device(
    inputs, w_qkv, w_gates, conv_weight, decay_rate, gate_bias, norm_gain, w_out, grad_out
):
    sequence = lax.all_gather(inputs[0], "tensor", axis=1, tiled=True)
    qkv_full, out_full = (
        lax.all_gather(w_qkv, "dp", axis=1, tiled=True),
        lax.all_gather(w_out, "dp", axis=1, tiled=True),
    )
    projected = jnp.einsum("ld,sdc->slc", sequence, qkv_full, preferred_element_type=jnp.float32)
    logits = jnp.einsum("ld,sdh->slh", sequence, w_gates, preferred_element_type=jnp.float32)
    core_out, pullback = jax.vjp(
        layer_core, projected, logits, conv_weight, decay_rate, gate_bias, norm_gain
    )
    core_low = core_out.astype(jnp.bfloat16)
    out_part = out_full
    output_cols = lax.psum_scatter(
        lax.dot_general(
            out_part, core_low, (((0,), (1,)), ((), ())), preferred_element_type=jnp.float32
        ).astype(jnp.bfloat16),
        "tensor",
        scatter_dimension=0,
        tiled=True,
    ).astype(jnp.float32)
    output = output_cols.T.astype(jnp.bfloat16)
    out_part = out_full
    core_grad = lax.dot_general(
        lax.all_gather(grad_out[0], "tensor", axis=1, tiled=True),
        out_part,
        (((1,), (1,)), ((), ())),
        preferred_element_type=jnp.float32,
    )
    proj_grad, logit_grad, conv_grad, rate_grad, bias_grad, gain_grad = pullback(core_grad)
    proj_low = proj_grad.astype(jnp.bfloat16)
    logit_low = logit_grad.astype(jnp.bfloat16)
    grad_cols = lax.psum_scatter(
        (
            jnp.einsum("slc,sdc->dl", proj_low, qkv_full, preferred_element_type=jnp.float32)
            + jnp.einsum("slh,sdh->dl", logit_low, w_gates, preferred_element_type=jnp.float32)
        ).astype(jnp.bfloat16),
        "tensor",
        scatter_dimension=0,
        tiled=True,
    ).astype(jnp.float32)
    grad_in = grad_cols.T.astype(jnp.bfloat16)
    gate_grad = jnp.einsum("ld,slh->sdh", sequence, logit_low, preferred_element_type=jnp.float32)
    grad_gates, grad_conv, grad_rate, grad_bias = lax.psum(
        (gate_grad, conv_grad, rate_grad, bias_grad), "dp"
    )
    grad_gain = lax.psum(gain_grad, ("dp", "tensor"))
    return (output[None], grad_in[None], grad_gates, grad_conv, grad_rate, grad_bias, grad_gain)


def solution(mesh):
    return jax.shard_map(
        on_device,
        mesh=mesh,
        in_specs=(
            P("dp", None, "tensor"),
            P(None, "dp", "tensor"),
            P(None, None, "tensor"),
            P(None, None, "tensor"),
            P("tensor"),
            P("tensor"),
            P(),
            P("tensor", "dp"),
            P("dp", None, "tensor"),
        ),
        out_specs=(
            P("dp", None, "tensor"),
            P("dp", None, "tensor"),
            P(None, None, "tensor"),
            P(None, None, "tensor"),
            P("tensor"),
            P("tensor"),
            P(),
        ),
        check_vma=False,
    )
```

profile of v0, /device:TPU:1, one launch (start us, length us, event | category | flops | bytes accessed | tf_op | source)
XLA Modules:
  0.0 764.9 jit_solution(5583303401060211434)
XLA Ops:
  13.1 63.4 %all-gather.11.cloned.1.call-done = bf16[1,128,5120]{1,2,0:T(8,128)(2,1)} async-done(((bf16[1,128,320]{1,2,0:T(8,128)(2,1)}), bf16[1,128,5120]{1,2,0:T(8,128)(2,1)}) %all-gather.11.cloned.1.call-update) | async-done | bytes 1310736 | tf_op jit(solution)/shard_map/all_gather | solution.py:97
  76.5 1.7 fusion.180
  78.3 1.3 multiply_bitcast_fusion
  80.3 57.5 %all-gather.13.cloned.1.call-done = bf16[1,128,5120]{1,2,0:T(8,128)(2,1)} async-done(((bf16[1,128,320]{1,2,0:T(8,128)(2,1)}), bf16[1,128,5120]{1,2,0:T(8,128)(2,1)}) %all-gather.13.cloned.1.call-update) | async-done | bytes 1310736 | tf_op jit(solution)/shard_map/all_gather | solution.py:120
  137.7 69.0 %all-gather.9.cloned.1.call-done = bf16[256,5120]{0,1:T(8,128)(2,1)} async-done(((bf16[256,160]{0,1:T(8,128)(2,1)}), bf16[256,5120]{0,1:T(8,128)(2,1)}) %all-gather.9.cloned.1.call-update) | async-done | bytes 2621456 | tf_op jit(solution)/shard_map/all_gather | solution.py:100
  206.8 3.4 fusion.177
  210.2 72.8 %all-gather.7.cloned.1.call-done = bf16[3,5120,256]{2,1,0:T(8,128)(2,1)} async-done(((bf16[3,160,256]{2,1,0:T(8,128)(2,1)}), bf16[3,5120,256]{2,1,0:T(8,128)(2,1)}) %all-gather.7.cloned.1.call-update) | async-done | bytes 7864336 | tf_op jit(solution)/shard_map/all_gather | solution.py:99
  283.0 4.5 fusion.174
  294.8 66.1 %while.92 = (s32[]{:T(128)}, f32[2,128,128]{2,1,0:T(8,128)S(1)}, f32[2,2,64,128]{3,2,0,1:T(8,128)}, f32[2,2,64,64]{3,2,1,0:T(8,128)}, f32[2,2,128,64]{2,3,1,0:T(...) while((s32[]{:T(128)}, f32[2,128,128]{2,1,0:T(8,128)S(1)}, ...), condition=%wide.region_4.5_spmd.clone.clone, body=%wide.region_2.4_spmd.clone.clone.sunk | while | flops 126431552 | bytes 3592781 | solution.py:51
  300.7 1.9 bitcast_dynamic-update-slice_fusion.22
  302.9 1.4 add_bitcast_fusion.4
  304.4 11.2 %custom-call.51 = f32[2,1,64,64]{2,3,1,0:T(8,128)} custom-call(f32[2,1,64,64]{3,2,1,0:T(8,128)} %add_bitcast_fusion.4), custom_call_target="InvertDiagBlocksLowerTriangular" | custom-call | tf_op jit(solution)/shard_map/jvp(vmap())/while/body/eval_jaxpr/jit(_solve_triangular)/triangular_solve | solution.py:37
  315.6 1.2 bitcast_dynamic-update-slice_fusion.23
  316.8 1.2 convolution_add_fusion.17
  318.0 1.7 bitcast_dynamic-update-slice_fusion.25
  319.7 1.8 fusion.287
  321.5 1.4 bitcast_dynamic-update-slice_fusion.26
  322.9 1.3 constant_dynamic-update-slice_fusion.13
  324.2 1.3 constant_dynamic-update-slice_fusion.14
  325.6 1.2 dynamic_update_slice.344
  333.7 1.9 bitcast_dynamic-update-slice_fusion.22
  335.9 1.4 add_bitcast_fusion.4
  337.4 11.2 %custom-call.51 = f32[2,1,64,64]{2,3,1,0:T(8,128)} custom-call(f32[2,1,64,64]{3,2,1,0:T(8,128)} %add_bitcast_fusion.4), custom_call_target="InvertDiagBlocksLowerTriangular" | custom-call | tf_op jit(solution)/shard_map/jvp(vmap())/while/body/eval_jaxpr/jit(_solve_triangular)/triangular_solve | solution.py:37
  348.6 1.2 bitcast_dynamic-update-slice_fusion.23
  349.8 1.2 convolution_add_fusion.17
  351.0 1.7 bitcast_dynamic-update-slice_fusion.25
  352.7 1.8 fusion.287
  354.5 1.4 bitcast_dynamic-update-slice_fusion.26
  355.9 1.3 constant_dynamic-update-slice_fusion.13
  357.2 1.3 constant_dynamic-update-slice_fusion.14
  358.6 1.2 dynamic_update_slice.344
  359.7 1.2 constant_dynamic-update-slice_fusion.15
  362.0 1.7 fusion.191
  363.7 1.7 add_add_fusion.2
  366.4 2.0 fusion.166
  368.5 2.6 copy.176
  374.6 53.9 %while.93 = (s32[]{:T(128)}, f32[2,128,128]{2,1,0:T(8,128)S(1)}, f32[2,2,64,128]{3,2,0,1:T(8,128)}, f32[2,2,64,128]{3,2,0,1:T(8,128)}, f32[2,2,64,128]{3,2,0,1:T...) while((s32[]{:T(128)}, f32[2,128,128]{2,1,0:T(8,128)S(1)}, ...), condition=%wide.region_19.20_spmd.clone.clone, body=%wide.region_8.19_spmd.clone.clone.sunk | while | flops 258888384 | bytes 6239372 | solution.py:51
  380.9 9.8 %custom-call.52 = f32[2,1,64,64]{2,3,1,0:T(8,128)S(1)} custom-call(f32[2,1,64,64]{3,2,1,0:T(8,128)S(1)} %add_bitcast_fusion.5), custom_call_target="InvertDiagBlocksLowerTriangular" | custom-call | tf_op jit(solution)/shard_map/transpose(jvp(vmap()))/while/body/eval_jaxpr/jit(_solve_triangular)/triangular_solve | solution.py:37
  394.3 1.3 fusion.319
  407.9 9.8 %custom-call.52 = f32[2,1,64,64]{2,3,1,0:T(8,128)S(1)} custom-call(f32[2,1,64,64]{3,2,1,0:T(8,128)S(1)} %add_bitcast_fusion.5), custom_call_target="InvertDiagBlocksLowerTriangular" | custom-call | tf_op jit(solution)/shard_map/transpose(jvp(vmap()))/while/body/eval_jaxpr/jit(_solve_triangular)/triangular_solve | solution.py:37
  421.2 1.3 fusion.319
  437.2 1.3 multiply_reduce_fusion.3
  438.7 5.8 convolution_bitcast_fusion
  445.1 1.4 copy.178
  447.8 103.1 %all-reduce.18 = (f32[3,4,256]{2,0,1:T(4,128)S(1)}, f32[2]{0:T(128)}, f32[2]{0:T(128)}) all-reduce(f32[3,4,256]{2,0,1:T(4,128)S(1)} %pad_add_fusion.3, f32[2]{0:T(128)S(1)} %neg.81, f32[2]{0:T(128)S(1)} %get-tuple-element.2177), channel_id=1, replica_groups=mesh['dp'=32,'tensor'=16] {'dp'}, use_global_device_ids=true, to_apply=%region_28.29 | all-reduce | flops 3076 | bytes 24608 | tf_op jit(solution)/shard_map/psum | solution.py:139
  551.5 102.0 %psum.39 = f32[128]{0:T(128)} all-reduce(f32[128]{0:T(128)S(1)} %copy-done.42), channel_id=1, replica_groups=mesh['dp'=32,'tensor'=16] {'dp','tensor'}, use_global_device_ids=true, to_apply=%region_34.35 | all-reduce | flops 128 | bytes 1024 | tf_op jit(solution)/shard_map/psum | solution.py:142
  657.0 99.5 %all-reduce.21.cloned.1.call-done = f32[2,5120,2]{1,2,0:T(2,128)} async-done(((f32[2,5120,2]{1,2,0:T(2,128)}), f32[2,5120,2]{1,2,0:T(2,128)}) %all-reduce.21.cloned.1.call-update) | async-done | bytes 81936 | tf_op jit(solution)/shard_map/psum | solution.py:139
  756.5 1.5 copy.379
  (298 shorter events, 78.4 us)
Async XLA Ops:
  7.2 69.3 %copy-start = (bf16[2,5120,2]{1,2,0:T(2,128)(2,1)S(1)}, bf16[2,5120,2]{1,2,0:T(2,128)(2,1)}, u32[]{:S(2)}) copy-start(bf16[2,5120,2]{1,2,0:T(2,128)(2,1)} %param.15) | copy-start | bytes 122884
  7.2 69.3 %all-gather.11.cloned.1.call-start = ((), (), s32[]{:S(2)}) async-start(), calls=%async_computation.5 | async-start | bytes 1392640 | tf_op jit(solution)/shard_map/all_gather | solution.py:97
  7.9 129.8 %all-gather.13.cloned.1.call-start = ((), (), s32[]{:S(2)}) async-start(), calls=%async_computation.6 | async-start | bytes 1392640 | tf_op jit(solution)/shard_map/all_gather | solution.py:120
  8.7 198.1 %all-gather.9.cloned.1.call-start = ((), (), s32[]{:S(2)}) async-start(), calls=%async_computation.3 | async-start | bytes 2703360 | tf_op jit(solution)/shard_map/all_gather | solution.py:100
  9.4 273.6 %all-gather.7.cloned.1.call-start = ((), (), s32[]{:S(2)}) async-start(), calls=%async_computation.2 | async-start | bytes 8110080 | tf_op jit(solution)/shard_map/all_gather | solution.py:99
  10.0 643.5 %reduce-scatter.7.cloned.1.call-start = ((), (), s32[]{:S(2)}) async-start(), calls=%async_computation.7 | async-start | bytes 1392640
  10.9 199.3 %copy-start.41 = (f32[2]{0:T(128)}, f32[2]{0:T(128)S(1)}, u32[]{:S(2)}) copy-start(f32[2]{0:T(128)S(1)} %neg.74) | copy-start | bytes 28
  13.1 274.5 %copy-start.28 = (f32[3,256]{1,0:T(4,128)}, f32[3,256]{1,0:T(4,128)S(1)}, u32[]{:S(2)}) copy-start(f32[3,256]{1,0:T(4,128)S(1)} %get-tuple-element.2245) | copy-start | bytes 9220
  13.1 274.5 %copy-start.30 = (f32[3,256]{1,0:T(4,128)}, f32[3,256]{1,0:T(4,128)S(1)}, u32[]{:S(2)}) copy-start(f32[3,256]{1,0:T(4,128)S(1)} %get-tuple-element.2246) | copy-start | bytes 9220
  13.1 274.5 %copy-start.32 = (f32[3,256]{1,0:T(4,128)}, f32[3,256]{1,0:T(4,128)S(1)}, u32[]{:S(2)}) copy-start(f32[3,256]{1,0:T(4,128)S(1)} %get-tuple-element.2247) | copy-start | bytes 9220
  13.1 274.5 %copy-start.34 = (f32[3,256]{1,0:T(4,128)}, f32[3,256]{1,0:T(4,128)S(1)}, u32[]{:S(2)}) copy-start(f32[3,256]{1,0:T(4,128)S(1)} %get-tuple-element.2248) | copy-start | bytes 9220
  76.5 206.5 %copy-start.6 = (bf16[1,128,5120]{1,2,0:T(8,128)(2,1)S(1)}, bf16[1,128,5120]{1,2,0:T(8,128)(2,1)}, u32[]{:S(2)}) copy-start(bf16[1,128,5120]{1,2,0:T(8,128)(2,1)} %all-gather.11.cloned.1.call-done) | copy-start | bytes 3932164
  78.2 209.3 %copy-start.40 = (f32[2,128,2]{1,2,0:T(2,128)}, f32[2,128,2]{1,2,0:T(2,128)S(1)}, u32[]{:S(2)}) copy-start(f32[2,128,2]{1,2,0:T(2,128)S(1)} %fusion.180) | copy-start | bytes 6148
  292.8 2.0 copy-start.37
  294.8 71.6 %copy-start.1 = (bf16[256,5120]{0,1:T(8,128)(2,1)S(1)}, bf16[256,5120]{0,1:T(8,128)(2,1)}, u32[]{:S(2)}) copy-start(bf16[256,5120]{0,1:T(8,128)(2,1)} %all-gather.9.cloned.1.call-done) | copy-start | bytes 7864324
  298.0 4.5 copy-start.8
  298.8 3.8 copy-start.27
  300.0 2.9 copy-start.24
  300.7 1.9 copy-start.23
  331.1 4.5 copy-start.8
  331.9 3.7 copy-start.27
  333.0 2.9 copy-start.24
  333.7 1.9 copy-start.23
  368.4 6.1 copy-start.4
  368.4 6.1 copy-start.5
  368.4 6.1 copy-start.9
  368.4 6.1 copy-start.14
  368.4 6.1 copy-start.16
  368.4 6.1 copy-start.17
  368.5 6.1 copy-start.18
  368.5 6.1 copy-start.19
  368.5 6.1 copy-start.20
  368.5 6.1 copy-start.25
  371.1 284.1 %reduce-scatter.9.cloned.1.call-start = ((), (), s32[]{:S(2)}) async-start(), calls=%async_computation.8 | async-start | bytes 1392640
  374.5 55.5 %copy-start.13 = (f32[128,2,128]{2,1,0:T(2,128)S(1)}, f32[128,2,128]{2,1,0:T(2,128)}, u32[]{:S(2)}) copy-start(f32[128,2,128]{2,1,0:T(2,128)} %copy-done.12) | copy-start | bytes 393220
  374.6 56.7 %copy-start.11 = (f32[128,2,128]{2,1,0:T(2,128)S(1)}, f32[128,2,128]{2,1,0:T(2,128)}, u32[]{:S(2)}) copy-start(f32[128,2,128]{2,1,0:T(2,128)} %copy-done.10) | copy-start | bytes 393220
  374.6 62.6 %copy-start.3 = (f32[3,128,256]{2,1,0:T(8,128)S(1)}, f32[3,128,256]{2,1,0:T(8,128)}, u32[]{:S(2)}) copy-start(f32[3,128,256]{2,1,0:T(8,128)} %copy-done.2) | copy-start | bytes 1179652
  374.6 62.6 %copy-start.15 = (f32[3,128,256]{2,1,0:T(8,128)S(1)}, f32[3,128,256]{2,1,0:T(8,128)}, u32[]{:S(2)}) copy-start(f32[3,128,256]{2,1,0:T(8,128)} %get-tuple-element.2181) | copy-start | bytes 1179652
  380.9 16.0 %copy-start.26 = (f32[2,64]{1,0:T(2,128)S(1)}, f32[2,64]{1,0:T(2,128)}, u32[]{:S(2)}) copy-start(f32[2,64]{1,0:T(2,128)} %get-tuple-element.2730) | copy-start | bytes 1540 | tf_op jit(solution)/shard_map/transpose(jvp(vmap()))/while
  390.7 5.1 copy-start.21
  407.8 16.0 %copy-start.26 = (f32[2,64]{1,0:T(2,128)S(1)}, f32[2,64]{1,0:T(2,128)}, u32[]{:S(2)}) copy-start(f32[2,64]{1,0:T(2,128)} %get-tuple-element.2730) | copy-start | bytes 1540 | tf_op jit(solution)/shard_map/transpose(jvp(vmap()))/while
  417.7 5.1 copy-start.21
  428.5 9.9 %copy-start.29 = (f32[3,256]{1,0:T(4,128)S(1)}, f32[3,256]{1,0:T(4,128)}, u32[]{:S(2)}) copy-start(f32[3,256]{1,0:T(4,128)} %copy-done.28) | copy-start | bytes 9220
  428.5 9.9 %copy-start.31 = (f32[3,256]{1,0:T(4,128)S(1)}, f32[3,256]{1,0:T(4,128)}, u32[]{:S(2)}) copy-start(f32[3,256]{1,0:T(4,128)} %copy-done.30) | copy-start | bytes 9220
  428.5 9.9 %copy-start.33 = (f32[3,256]{1,0:T(4,128)S(1)}, f32[3,256]{1,0:T(4,128)}, u32[]{:S(2)}) copy-start(f32[3,256]{1,0:T(4,128)} %copy-done.32) | copy-start | bytes 9220
  428.5 10.0 %copy-start.35 = (f32[3,256]{1,0:T(4,128)S(1)}, f32[3,256]{1,0:T(4,128)}, u32[]{:S(2)}) copy-start(f32[3,256]{1,0:T(4,128)} %copy-done.34) | copy-start | bytes 9220
  445.1 106.4 %copy-start.42 = (f32[128]{0:T(128)S(1)}, f32[128]{0:T(128)}, u32[]{:S(2)}) copy-start(f32[128]{0:T(128)} %get-tuple-element.2038) | copy-start | bytes 1540
  446.6 310.0 %all-reduce.21.cloned.1.call-start = ((), (), s32[]{:S(2)}) async-start(), calls=%async_computation.4 | async-start | bytes 163840 | tf_op jit(solution)/shard_map/psum | solution.py:139
  (9 other events, 7.6 us)
Sparse Core Ops, SparseCore 0:
  11.0 65.3 all-gather.10
  79.5 58.2 all-gather.12
  139.9 66.8 all-gather.8
  208.7 74.2 all-gather.6
  371.2 90.2 reduce-scatter.6
  465.4 90.2 reduce-scatter.8
  559.2 197.2 all-reduce.20
where the time goes:
time: 767 us; the launch traced here: 765 us
  waiting for transfers between devices  365 us (48%)
  blocking collectives  205 us (27%)
  other arithmetic  83.8 us (11%)
  matrix products  53.8 us (7%)
  local copies, waits for them, and re-layouts  41.6 us (5%)
  between operations  14.9 us (2%)
    psum x1, blocking collectives, on_device(): lax.psum((gate_grad, conv_grad, rate_grad, bias_grad), 'dp')  103 us
    psum x1, blocking collectives, on_device(): grad_gain = lax.psum(gain_grad, ('dp', 'tensor'))  102 us
    psum x1, waiting for transfers between devices, on_device(): lax.psum((gate_grad, conv_grad, rate_grad, bias_grad), 'dp')  99.5 us
    all_gather x1, waiting for transfers between devices, on_device(): lax.all_gather(w_qkv, 'dp', axis=1, tiled=True)  72.8 us
    all_gather x1, waiting for transfers between devices, on_device(): lax.all_gather(w_out, 'dp', axis=1, tiled=True)  69 us
    all_gather x1, waiting for transfers between devices, on_device(): sequence = lax.all_gather(inputs[0], 'tensor', axis=1, tiled=True)  63.4 us
    all_gather x1, waiting for transfers between devices, on_device(): lax.all_gather(grad_out[0], 'tensor', axis=1, tiled=True)  57.5 us
    another operation x20, other arithmetic, advance(): jax.scipy.linalg.solve_triangular(system, target, lower=True, unit_diagon...  45.3 us
  transfers between devices with their start and end apart: 7, of which 5 were waited for; matrix products, arithmetic and copies ran while one was open for 12% of the time, Pallas kernels for 0%

commit v1 on v0

v1 whole, which is shorter than its diff:
```python
import functools
import math

import jax
import jax.numpy as jnp
from jax import lax
from jax.experimental import pallas as pl
from jax.experimental.pallas import tpu as pltpu
from jax.sharding import PartitionSpec as P

MESH = pl.DeviceIdType.MESH
F32, BF16 = jnp.float32, jnp.bfloat16
LEN = 128
HEAD = 128
TAPS = 4
CORES = 2
ZL = 2
NN = (((1,), (0,)), ((), ()))
NT = (((1,), (1,)), ((), ()))


class Place:
    def __init__(self, dp, tensor):
        self.ny = dp // (ZL * CORES)
        self.nz = 4 if tensor == 16 else 2
        self.nx = tensor // self.nz
        d, t = lax.axis_index("dp"), lax.axis_index("tensor")
        self.d, self.t = d, t
        self.zl = d // (self.ny * CORES)
        self.y = (d // CORES) % self.ny
        self.c = d % CORES
        self.zh = t // self.nx
        self.x = t % self.nx

    def dp_of(self, zl, y, c):
        return zl * (self.ny * CORES) + y * CORES + c

    def at_y(self, step):
        return self.dp_of(self.zl, (self.y + step + self.ny) % self.ny, self.c), self.t

    def at_z(self):
        return self.dp_of(1 - self.zl, self.y, self.c), self.t

    def at_core(self):
        return self.dp_of(self.zl, self.y, 1 - self.c), self.t

    def at_zh(self, step):
        return self.d, ((self.zh + step + self.nz) % self.nz) * self.nx + self.x

    def at_x(self, step):
        return self.d, self.zh * self.nx + (self.x + step + self.nx) % self.nx


def remote(src, dst, send, recv, where):
    return pltpu.make_async_remote_copy(
        src_ref=src, dst_ref=dst, send_sem=send, recv_sem=recv, device_id=where, device_id_type=MESH
    )


def meet(peers):
    barrier = pltpu.get_barrier_semaphore()
    for where in peers:
        pl.semaphore_signal(barrier, inc=1, device_id=where, device_id_type=MESH)
    pl.semaphore_wait(barrier, len(peers))


def gather_kernel(
    dp, tensor, w_ref, x_ref, g_ref, wf_ref, xf_ref, gf_ref, own_sem,
    yp_s, yp_r, ym_s, ym_r, z_s, z_r, c_s, c_r, t1_s, t1_r, t2_s, t2_r,
):
    here = Place(dp, tensor)
    ny, nz, nx = here.ny, here.nz, here.nx
    far = ny // 2
    shard = w_ref.shape[1]
    half = shard // 2
    meet(
        [here.at_y(1), here.at_y(-1), here.at_z(), here.at_core()]
        + [here.at_zh(s) for s in range(1, nz)]
        + [here.at_x(s) for s in range(1, nx)]
    )

    def block(zl, y, c, h):
        row = pl.multiple_of(here.dp_of(zl, y, c) * shard + h * half, 16)
        return wf_ref.at[:, pl.ds(row, half), :]

    own = [
        pltpu.make_async_copy(w_ref, wf_ref.at[:, pl.ds(pl.multiple_of(here.d * shard, 16), shard), :], own_sem.at[0]),
        pltpu.make_async_copy(x_ref, xf_ref.at[here.t], own_sem.at[1]),
        pltpu.make_async_copy(g_ref, gf_ref.at[here.t], own_sem.at[2]),
    ]
    for copy in own:
        copy.start()
    sent = []

    def send(src, dst, s, r, where):
        copy = remote(src, dst, s, r, where)
        copy.start()
        sent.append(copy)

    def arrive(dst, s, r):
        remote(dst, dst, s, r, here.at_core()).wait_recv()

    def travels(direction, k, h):
        return k < far or (k == far and h == (0 if direction > 0 else 1))

    def y_sems(direction):
        return (yp_s, yp_r) if direction > 0 else (ym_s, ym_r)

    def on_y(src, dst, direction, k, p, h):
        if k <= far and travels(direction, k, h):
            s, r = y_sems(direction)
            send(src, dst, s.at[k - 1, p, h], r.at[k - 1, p, h], here.at_y(direction))

    mine = [w_ref.at[:, pl.ds(h * half, half), :] for h in range(2)]
    for h in range(2):
        dst = block(here.zl, here.y, here.c, h)
        send(mine[h], dst, z_s.at[h], z_r.at[h], here.at_z())
        on_y(mine[h], dst, 1, 1, 0, h)
        on_y(mine[h], dst, -1, 1, 0, h)
    arrays = ((x_ref, xf_ref), (g_ref, gf_ref))
    for a, (src, dst) in enumerate(arrays):
        for s in range(1, nz):
            send(src, dst.at[here.t], t1_s.at[s - 1, a], t1_r.at[s - 1, a], here.at_zh(s))
    for a, (src, dst) in enumerate(arrays):
        for s in range(1, nx):
            send(src, dst.at[here.t], t2_s.at[s - 1, 0, a], t2_r.at[s - 1, 0, a], here.at_x(s))
    for h in range(2):
        dst = block(here.zl, here.y, here.c, h)
        send(mine[h], dst, c_s.at[0, 0, h], c_r.at[0, 0, h], here.at_core())
    for h in range(2):
        got = block(1 - here.zl, here.y, here.c, h)
        arrive(got, z_s.at[h], z_r.at[h])
        on_y(got, got, 1, 1, 1, h)
        on_y(got, got, -1, 1, 1, h)
        send(got, got, c_s.at[1, 0, h], c_r.at[1, 0, h], here.at_core())

    def activations():
        for s in range(1, nz):
            t = ((here.zh - s + nz) % nz) * nx + here.x
            for a, (_, dst) in enumerate(arrays):
                arrive(dst.at[t], t1_s.at[s - 1, a], t1_r.at[s - 1, a])
                for sx in range(1, nx):
                    send(dst.at[t], dst.at[t], t2_s.at[sx - 1, s, a], t2_r.at[sx - 1, s, a], here.at_x(sx))

    for k in range(1, far + 1):
        for p in range(2):
            zl = here.zl if p == 0 else 1 - here.zl
            for h in range(2):
                for direction in (1, -1):
                    if not travels(direction, k, h):
                        continue
                    y = (here.y - direction * k + ny) % ny
                    got = block(zl, y, here.c, h)
                    s, r = y_sems(direction)
                    arrive(got, s.at[k - 1, p, h], r.at[k - 1, p, h])
                    on_y(got, got, direction, k + 1, p, h)
                    place = k if direction > 0 else ny - k
                    send(got, got, c_s.at[p, place, h], c_r.at[p, place, h], here.at_core())
        if k == 1:
            activations()
    for sx in range(1, nx):
        for s in range(nz):
            t = ((here.zh - s + nz) % nz) * nx + (here.x - sx + nx) % nx
            for a, (_, dst) in enumerate(arrays):
                arrive(dst.at[t], t2_s.at[sx - 1, s, a], t2_r.at[sx - 1, s, a])
    for p in range(2):
        zl = here.zl if p == 0 else 1 - here.zl
        for place in range(ny):
            y = (here.y - place + ny) % ny
            for h in range(2):
                arrive(block(zl, y, 1 - here.c, h), c_s.at[p, place, h], c_r.at[p, place, h])
    for copy in own:
        copy.wait()
    for copy in sent:
        copy.wait_send()


def gather(dp, tensor, w, x, g):
    ny = dp // (ZL * CORES)
    nz = 4 if tensor == 16 else 2
    nx = tensor // nz
    dma = pltpu.SemaphoreType.DMA
    sems = []
    for dims in ((ny // 2, 2, 2), (ny // 2, 2, 2), (2,), (2, ny, 2), (nz - 1, 2), (nx - 1, nz, 2)):
        sems += [dma(dims), dma(dims)]
    any_spec = pl.BlockSpec(memory_space=pl.ANY)
    return pl.pallas_call(
        functools.partial(gather_kernel, dp, tensor),
        name="gather",
        out_shape=(
            jax.ShapeDtypeStruct((w.shape[0], dp * w.shape[1], w.shape[2]), BF16),
            jax.ShapeDtypeStruct((tensor,) + x.shape, BF16),
            jax.ShapeDtypeStruct((tensor,) + g.shape, BF16),
        ),
        in_specs=[any_spec] * 3,
        out_specs=(any_spec,) * 3,
        scratch_shapes=[dma((3,))] + sems,
        compiler_params=pltpu.CompilerParams(collective_id=0, has_side_effects=True),
    )(w, x, g)


def halves(a):
    high = a.astype(BF16)
    return high, (a - high.astype(F32)).astype(BF16)


def dot(a, b, dims=NN):
    return lax.dot_general(a, b, dims, preferred_element_type=F32)


def product(a, b, dims=NN):
    ah, al = halves(a)
    bh, bl = halves(b)
    side = 0 if dims is NN else 1
    return dot(jnp.concatenate([ah, ah, al], 1), jnp.concatenate([bh, bl, bh], side), dims)


def triangle_product(triangle, a):
    high = a.astype(BF16)
    rest = a - high.astype(F32)
    mid = rest.astype(BF16)
    low = (rest - mid.astype(F32)).astype(BF16)
    return dot(jnp.concatenate([triangle] * 3, 1), jnp.concatenate([high, mid, low], 0))


def unit_inverse(lower, xor):
    inverse = jnp.where(xor == 0, 1.0, 0.0) - jnp.where(xor == 1, lower, 0.0)
    width = 2
    while width < lower.shape[0]:
        between = jnp.where((xor >= width) & (xor < 2 * width), lower, 0.0)
        inverse = inverse - product(product(inverse, between), inverse)
        width *= 2
    return inverse


def head_forward(q, k, v, beta, c_col, c_row, within, strict, xor):
    fading = jnp.where(within, jnp.exp(jnp.where(within, c_col - c_row, 0.0)), 0.0)
    faded_keys = jnp.where(strict, fading * product(k, k, NT), 0.0)
    lower = beta * faded_keys
    inverse = unit_inverse(lower, xor)
    rows = product(inverse, beta * v)
    scores = fading * product(q, k, NT)
    return fading, faded_keys, lower, inverse, rows, scores, product(scores, rows)


def head_backward(q, k, v, beta, fading, faded_keys, lower, inverse, rows, scores, d_out, within, strict):
    d_scores = jnp.where(within, product(d_out, rows, NT), 0.0)
    d_rows = product(scores.T, d_out)
    d_target = product(inverse.T, d_rows)
    d_lower = jnp.where(strict, -product(d_target, rows, NT), 0.0)
    faded = fading * d_scores
    both = beta * fading * d_lower
    dq = product(faded, k)
    dk = product(faded.T, q) + product(both + both.T, k)
    dv = beta * d_target
    spread = d_scores * scores + d_lower * lower
    dc = jnp.sum(spread - spread.T, 1, keepdims=True)
    d_beta = jnp.sum(d_lower * faded_keys + d_target * v, 1, keepdims=True)
    return dq, dk, dv, dc, d_beta


def shifted(a, step, row):
    if step == 0:
        return a
    size = a.shape[0]
    moved = pltpu.roll(a, step % size, 0)
    keep = row >= step if step > 0 else row < size + step
    return jnp.where(keep, moved, 0.0)


def core_kernel(wf_ref, xf_ref, gf_ref, wg_ref, conv_ref, small_ref, core_ref, low_ref, pack_ref, gain_ref, proj, back):
    slots, _, part = xf_ref.shape
    width = wf_ref.shape[2]

    proj[...] = jnp.zeros_like(proj)
    back[...] = jnp.zeros_like(back)

    def contract(i, _):
        rows = pl.ds(pl.multiple_of(i * part, 64), part)
        x, g = xf_ref[i], gf_ref[i]
        for s in range(3):
            proj[:, s * width : (s + 1) * width] += dot(x, wf_ref[s, rows, :])
        proj[:, 3 * width :] += dot(x, wg_ref[rows, :])
        back[...] += dot(g, wf_ref[3, rows, :])
        return 0

    lax.fori_loop(0, slots, contract, 0)

    row = lax.broadcasted_iota(jnp.int32, (LEN, LEN), 0)
    lane = lax.broadcasted_iota(jnp.int32, (LEN, LEN), 1)
    wide_row = lax.broadcasted_iota(jnp.int32, (LEN, width), 0)
    within, strict, xor = row >= lane, row > lane, row ^ lane
    triangle = jnp.where(within, 1.0, 0.0).astype(BF16)
    triangle_t = jnp.where(row <= lane, 1.0, 0.0).astype(BF16)

    rate, bias, gain = small_ref[0:1, :], small_ref[1:2, :], small_ref[2:3, :]
    logits = proj[:, 3 * width :]
    pre = logits + bias
    soft = jnp.maximum(pre, 0.0) + jnp.log1p(jnp.exp(-jnp.abs(pre)))
    strength = 1.0 / (1.0 + jnp.exp(-logits))
    cumulative = triangle_product(triangle, -rate * soft)
    cumulative_t = cumulative.T

    before, gate, active = [], [], []
    for s in range(3):
        p = proj[:, s * width : (s + 1) * width]
        z = jnp.zeros_like(p)
        for i in range(TAPS):
            z = z + conv_ref[s * TAPS + i : s * TAPS + i + 1, :] * shifted(p, TAPS - 1 - i, wide_row)
        sigma = 1.0 / (1.0 + jnp.exp(-z))
        before.append(z)
        gate.append(sigma)
        active.append(z * sigma)

    heads = width // HEAD
    d_active = [[None] * heads for _ in range(3)]
    dc_all = jnp.zeros((LEN, LEN), F32)
    db_all = jnp.zeros((LEN, LEN), F32)
    gain_grad = jnp.zeros((1, HEAD), F32)
    for h in range(heads):
        cut = slice(h * HEAD, (h + 1) * HEAD)
        aq, ak, v = active[0][:, cut], active[1][:, cut], active[2][:, cut]
        nq = lax.rsqrt(jnp.sum(aq * aq, 1, keepdims=True) + 1e-6)
        nk = lax.rsqrt(jnp.sum(ak * ak, 1, keepdims=True) + 1e-6)
        uq, k = aq * nq, ak * nk
        scale = 1.0 / math.sqrt(HEAD)
        q = uq * scale
        beta = strength[:, heads + h : heads + h + 1]
        kept = head_forward(q, k, v, beta, cumulative[:, h : h + 1], cumulative_t[h : h + 1, :], within, strict, xor)
        out = kept[-1]
        r = lax.rsqrt(jnp.mean(out * out, 1, keepdims=True) + 1e-5)
        normed = out * r
        core_ref[:, cut] = (normed * gain).astype(BF16)
        d_core = back[:, cut]
        gain_grad = gain_grad + jnp.sum(d_core * normed, 0, keepdims=True)
        dn = d_core * gain
        d_out = r * (dn - normed * jnp.mean(dn * normed, 1, keepdims=True))
        dq, dk, dv, dc, d_beta = head_backward(q, k, v, beta, *kept[:-1], d_out, within, strict)
        dq = dq * scale
        d_active[0][h] = nq * (dq - uq * jnp.sum(uq * dq, 1, keepdims=True))
        d_active[1][h] = nk * (dk - k * jnp.sum(k * dk, 1, keepdims=True))
        d_active[2][h] = dv
        dc_all = jnp.where(lane == h, dc, dc_all)
        db_all = jnp.where(lane == heads + h, d_beta, db_all)

    pack_ref[...] = jnp.zeros_like(pack_ref)
    gain_ref[...] = jnp.zeros_like(gain_ref)
    gain_ref[0:1, :] = gain_grad
    gate_tiles = slots * pl.cdiv(part, 128) // 2

    for s in range(3):
        z, sigma = before[s], gate[s]
        dz = jnp.concatenate(d_active[s], 1) * (sigma * (1.0 + z * (1.0 - sigma)))
        p = proj[:, s * width : (s + 1) * width]
        dp = jnp.zeros_like(p)
        for i in range(TAPS):
            step = TAPS - 1 - i
            tap = conv_ref[s * TAPS + i : s * TAPS + i + 1, :]
            ahead = shifted(dz, -step, wide_row)
            dp = dp + tap * ahead
            total = jnp.sum(ahead * p, 0, keepdims=True)
            for j in range(width // 128):
                at = j * TAPS + i
                pack_ref[gate_tiles + s, at : at + 1, :] = total[:, j * 128 : (j + 1) * 128]
        low_ref[:, s * width : (s + 1) * width] = dp.astype(BF16)

    d_decay = triangle_product(triangle_t, dc_all)
    d_pre = -rate * d_decay / (1.0 + jnp.exp(-pre))
    pack_ref[gate_tiles + 3, 1:2, :] = jnp.sum(-soft * d_decay, 0, keepdims=True)
    pack_ref[gate_tiles + 3, 2:3, :] = jnp.sum(d_pre, 0, keepdims=True)
    d_logits = (d_pre + db_all * strength * (1.0 - strength)).astype(BF16)
    low_ref[:, 3 * width :] = d_logits
    d_logits_t = d_logits.astype(F32).T[0:16, :].astype(BF16)

    tiles = pl.cdiv(part, 128)

    def gates(i, _):
        for j in range(2):
            grad = dot(d_logits_t, xf_ref[2 * i + j])
            for n in range(tiles):
                at = j * tiles + n
                wide = min(128, part - n * 128)
                piece = grad[0:4, n * 128 : n * 128 + wide]
                pack_ref[i * tiles + at // 2, (at % 2) * 4 : (at % 2) * 4 + 4, 0:wide] = piece
        return 0

    lax.fori_loop(0, slots // 2, gates, 0)


def pack_tiles(dp, slots, part):
    ny = dp // (ZL * CORES)
    gate_tiles = slots * pl.cdiv(part, 128) // 2
    return gate_tiles, pl.cdiv(gate_tiles + 4, ny) * ny


def core(dp, wf, xf, gf, wg, conv, small):
    slots, _, part = xf.shape
    width = wf.shape[2]
    tiles = pack_tiles(dp, slots, part)[1]
    vmem = pl.BlockSpec(memory_space=pltpu.VMEM)
    return pl.pallas_call(
        core_kernel,
        name="core",
        out_shape=(
            jax.ShapeDtypeStruct((LEN, width), BF16),
            jax.ShapeDtypeStruct((LEN, 3 * width + 128), BF16),
            jax.ShapeDtypeStruct((tiles, 8, 128), F32),
            jax.ShapeDtypeStruct((8, 128), F32),
        ),
        in_specs=[vmem] * 6,
        out_specs=(vmem,) * 4,
        scratch_shapes=[pltpu.VMEM((LEN, 3 * width + 128), F32), pltpu.VMEM((LEN, width), F32)],
        compiler_params=pltpu.CompilerParams(vmem_limit_bytes=56 * 2**20),
    )(wf, xf, gf, wg, conv, small)


def reduce_kernel(
    dp, tensor, tiles_before, wf_ref, wg_ref, core_ref, low_ref, pack_ref, gain_ref, out_ref, gin_ref, sum_ref,
    parts, r1, keep, r2, gx, gz, mine, ry, rz, fin, all_sums,
    s1s, s1r, s2s, s2r, gxs, gxr, gzs, gzr, rys, ryr, rzs, rzr, ays, ayr,
):
    here = Place(dp, tensor)
    ny, nz, nx = here.ny, here.nz, here.nx
    part = out_ref.shape[0]
    width = core_ref.shape[1]
    each = pack_ref.shape[0] // ny
    q = here.zl * CORES + here.c

    def at_q(r):
        other = q ^ r
        return here.dp_of(other // CORES, here.y, other % CORES), here.t

    meet(
        [here.at_y(s) for s in range(1, ny)]
        + [at_q(r) for r in range(1, 4)]
        + [here.at_zh(s) for s in range(1, nz)]
        + [here.at_x(s) for s in range(1, nx)]
    )
    sent = []

    def send(src, dst, s, r, where):
        copy = remote(src, dst, s, r, where)
        copy.start()
        sent.append(copy)

    def arrive(dst, s, r):
        remote(dst, dst, s, r, here.at_core()).wait_recv()

    def back_of(step, size, now):
        return (now - step + size) % size

    gx[here.x] = gain_ref[...]
    for s in range(1, nx):
        send(gain_ref, gx.at[here.x], gxs.at[s - 1], gxr.at[s - 1], here.at_x(s))

    def first(a, build):
        def piece(i, _):
            sx, zh = (i // nz + 1) % nx, i % nz
            x = (here.x + sx) % nx
            t = zh * nx + x
            parts[a, t] = build(pl.ds(pl.multiple_of(t * part, 64), part)).astype(BF16)

            @pl.when(sx != 0)
            def _():
                remote(parts.at[a, t], r1.at[a, sx, zh], s1s.at[a, sx, zh], s1r.at[a, sx, zh], (here.d, here.zh * nx + x)).start()

            return 0

        lax.fori_loop(0, nx * nz, piece, 0)

    def second(a):
        for sz in [*range(1, nz), 0]:
            zh = (here.zh + sz) % nz
            total = parts[a, zh * nx + here.x].astype(F32)
            for sx in range(1, nx):
                arrive(r1.at[a, sx, zh], s1s.at[a, sx, zh], s1r.at[a, sx, zh])
                total = total + r1[a, sx, zh].astype(F32)
            if sz:
                mine[a, sz] = total.astype(BF16)
                send(mine.at[a, sz], r2.at[a, sz], s2s.at[a, sz], s2r.at[a, sz], here.at_zh(sz))
            else:
                keep[a] = total

    def last(a, ref):
        total = keep[a]
        for sz in range(1, nz):
            arrive(r2.at[a, sz], s2s.at[a, sz], s2r.at[a, sz])
            total = total + r2[a, sz].astype(F32)
        ref[...] = total.astype(BF16)

    first(0, lambda rows: dot(wf_ref[3, rows, :], core_ref[...], NT))

    for s in range(1, nx):
        arrive(gx.at[back_of(s, nx, here.x)], gxs.at[s - 1], gxr.at[s - 1])
    gz[here.zh] = sum(gx[i] for i in range(nx))
    for s in range(1, nz):
        send(gz.at[here.zh], gz.at[here.zh], gzs.at[s - 1], gzr.at[s - 1], here.at_zh(s))

    def grad_in(rows):
        total = dot(wg_ref[rows, :], low_ref[:, 3 * width :], NT)
        for s in range(3):
            total = total + dot(wf_ref[s, rows, :], low_ref[:, s * width : (s + 1) * width], NT)
        return total

    first(1, grad_in)

    for s in range(1, nz):
        arrive(gz.at[back_of(s, nz, here.zh)], gzs.at[s - 1], gzr.at[s - 1])
    sum_ref[...] = pack_ref[...]
    gain_at = tiles_before + 3
    sum_ref[gain_at, 0:1, :] = sum(gz[i, 0:1, :] for i in range(nz))
    own = pl.ds(here.y * each, each)
    mark = len(sent)
    for s in range(1, ny):
        there = (here.y + s) % ny
        send(sum_ref.at[pl.ds(there * each, each)], ry.at[here.y], rys.at[s - 1], ryr.at[s - 1], here.at_y(s))
    ry[here.y] = sum_ref[own]
    leaving, sent[mark:] = sent[mark:], []

    second(0)

    for s in range(1, ny):
        arrive(ry.at[back_of(s, ny, here.y)], rys.at[s - 1], ryr.at[s - 1])
    rz[q] = sum(ry[i] for i in range(ny))
    for r in range(1, 4):
        send(rz.at[q], rz.at[q], rzs.at[r - 1], rzr.at[r - 1], at_q(r))

    last(0, out_ref)
    second(1)

    for r in range(1, 4):
        arrive(rz.at[q ^ r], rzs.at[r - 1], rzr.at[r - 1])
    fin[...] = sum(rz[i] for i in range(4))
    for s in range(1, ny):
        send(fin, all_sums.at[here.y], ays.at[s - 1], ayr.at[s - 1], here.at_y(s))
    all_sums[here.y] = fin[...]
    for s in range(1, ny):
        arrive(all_sums.at[back_of(s, ny, here.y)], ays.at[s - 1], ayr.at[s - 1])
    for copy in leaving:
        copy.wait_send()
    for i in range(ny):
        sum_ref[i * each : (i + 1) * each] = all_sums[i]

    last(1, gin_ref)

    def finished(i, _):
        sx, zh = i // nz + 1, i % nz
        for a in range(2):
            remote(parts.at[a, 0], r1.at[a, sx, zh], s1s.at[a, sx, zh], s1r.at[a, sx, zh], here.at_core()).wait_send()
        return 0

    lax.fori_loop(0, (nx - 1) * nz, finished, 0)
    for copy in sent:
        copy.wait_send()


def reduce(dp, tensor, wf, wg, core_low, low, pack, gain):
    ny = dp // (ZL * CORES)
    nz = 4 if tensor == 16 else 2
    nx = tensor // nz
    part = wf.shape[1] // tensor
    each = pack.shape[0] // ny
    vmem = pl.BlockSpec(memory_space=pltpu.VMEM)
    dma = pltpu.SemaphoreType.DMA
    sems = []
    for dims in ((2, nx, nz), (2, nz), (nx - 1,), (nz - 1,), (ny - 1,), (3,), (ny - 1,)):
        sems += [dma(dims), dma(dims)]
    gate_tiles = pack_tiles(dp, tensor, part)[0]
    return pl.pallas_call(
        functools.partial(reduce_kernel, dp, tensor, gate_tiles),
        name="reduce",
        out_shape=(
            jax.ShapeDtypeStruct((part, LEN), BF16),
            jax.ShapeDtypeStruct((part, LEN), BF16),
            jax.ShapeDtypeStruct(pack.shape, F32),
        ),
        in_specs=[vmem] * 6,
        out_specs=(vmem,) * 3,
        scratch_shapes=[
            pltpu.VMEM((2, tensor, part, LEN), BF16),
            pltpu.VMEM((2, nx, nz, part, LEN), BF16),
            pltpu.VMEM((2, part, LEN), F32),
            pltpu.VMEM((2, nz, part, LEN), BF16),
            pltpu.VMEM((nx, 8, 128), F32),
            pltpu.VMEM((nz, 8, 128), F32),
            pltpu.VMEM((2, nz, part, LEN), BF16),
            pltpu.VMEM((ny, each, 8, 128), F32),
            pltpu.VMEM((4, each, 8, 128), F32),
            pltpu.VMEM((each, 8, 128), F32),
            pltpu.VMEM((ny, each, 8, 128), F32),
        ]
        + sems,
        compiler_params=pltpu.CompilerParams(collective_id=1, has_side_effects=True, vmem_limit_bytes=56 * 2**20),
    )(wf, wg, core_low, low, pack, gain)


def on_device(dp, tensor, inputs, w_qkv, w_gates, conv_weight, decay_rate, gate_bias, norm_gain, w_out, grad_out):
    part, slots = inputs.shape[2], tensor
    heads = decay_rate.shape[0]
    width = w_qkv.shape[2]
    shards = jnp.concatenate([w_qkv, w_out.T[None]], 0)
    wg = jnp.pad(jnp.moveaxis(w_gates, 0, 1).reshape(-1, 2 * heads), ((0, 0), (0, 128 - 2 * heads)))
    small = jnp.stack([jnp.pad(decay_rate, (0, 128 - heads)), jnp.pad(gate_bias, (0, 128 - heads)), norm_gain])
    small = jnp.pad(small, ((0, 5), (0, 0)))
    conv = conv_weight.reshape(3 * TAPS, width)
    wf, xf, gf = gather(dp, tensor, shards, inputs[0], grad_out[0])
    core_low, low, pack, gain = core(dp, wf, xf, gf, wg, conv, small)
    out, grad_in, total = reduce(dp, tensor, wf, wg, core_low, low, pack, gain)
    tiles = pl.cdiv(part, 128)
    count = pack_tiles(dp, slots, part)[0]
    gates = total[:count].reshape(slots, tiles, 4, 128)[:, :, : 2 * heads]
    gates = gates.transpose(2, 0, 1, 3).reshape(2, heads, slots, tiles * 128)[..., :part]
    grad_gates = gates.reshape(2, heads, slots * part).transpose(0, 2, 1)
    taps = total[count : count + 3].reshape(3, width // 128, TAPS, 128)
    grad_conv = taps.transpose(0, 2, 1, 3).reshape(3, TAPS, width)
    rest = total[count + 3]
    return (out.T[None], grad_in.T[None], grad_gates, grad_conv, rest[1, :heads], rest[2, :heads], rest[0])


def solution(mesh):
    dp, tensor = mesh.shape["dp"], mesh.shape["tensor"]
    return jax.shard_map(
        functools.partial(on_device, dp, tensor),
        mesh=mesh,
        in_specs=(
            P("dp", None, "tensor"),
            P(None, "dp", "tensor"),
            P(None, None, "tensor"),
            P(None, None, "tensor"),
            P("tensor"),
            P("tensor"),
            P(),
            P("tensor", "dp"),
            P("dp", None, "tensor"),
        ),
        out_specs=(
            P("dp", None, "tensor"),
            P("dp", None, "tensor"),
            P(None, None, "tensor"),
            P(None, None, "tensor"),
            P("tensor"),
            P("tensor"),
            P(),
        ),
        check_vma=False,
    )
```

time: 767 us -> 162 us (0.21)
  waiting for transfers between devices: 365 us -> 0 us
  blocking collectives: 205 us -> 0 us
  Pallas kernels: 0 us -> 141 us
  other arithmetic: 83.8 us -> 2.99 us
  matrix products: 53.8 us -> 0 us
  local copies, waits for them, and re-layouts: 41.6 us -> 16.5 us
  between operations: 14.9 us -> 0.67 us
    all_gather x4 -> x0, waiting for transfers between devices: 263 us -> none  [the longest x1 72.8 us: on_device(): lax.all_gather(w_qkv, 'dp', axis=1, tiled=True)]
    psum x2 -> x0, blocking collectives: 205 us -> none  [the longest x1 103 us: on_device(): lax.psum((gate_grad, conv_grad, rate_grad, bias_grad), 'dp')]
    pallas_call x0 -> x3, Pallas kernels: none -> 141 us  [the longest x1 71.4 us: gather(): pl.pallas_call(functools.partial(gather_kernel, dp, tensor), name='gather...]
    psum x1 -> x0, waiting for transfers between devices: 99.5 us -> none  [on_device(): lax.psum((gate_grad, conv_grad, rate_grad, bias_grad), 'dp')]
    dot_general x45 -> x0, matrix products: 47 us -> none  [the longest x6 6.54 us: advance(): jnp.dot((update_rows * remain).T, key_part, precision=HI)]
    another operation x46 -> x1, other arithmetic: 48.3 us -> 1.26 us  [on_device(): jnp.stack([jnp.pad(decay_rate, (0, 128 - heads)), jnp.pad(gate_bias, (0,...]
    dynamic_update_slice x12 -> x0, other arithmetic: 11.9 us -> none  [head_scan(): lax.scan(advance, initial, (to_blocks(queries), to_blocks(key_rows), to_b...]
    reduce_sum x16 -> x0, other arithmetic: 10.9 us -> none  [the longest x1 1.68 us: layer_core(): normed = heads_out / row_scale * norm_gain]
  transfers between devices with their start and end apart: 7 -> 0, of which waited for: 5 -> 0; matrix products, arithmetic and copies ran while one was open for 12% -> 0% of each run, Pallas kernels for 0% -> 0%
where the time goes in v1:
time: 162 us; the launch traced here: 161 us
  Pallas kernels  141 us (87%)
  local copies, waits for them, and re-layouts  16.5 us (10%)
  other arithmetic  2.99 us (2%)
    pallas_call x1, Pallas kernels, gather(): pl.pallas_call(functools.partial(gather_kernel, dp, tensor), name='gather...  71.4 us
    pallas_call x1, Pallas kernels, reduce(): pl.pallas_call(functools.partial(reduce_kernel, dp, tensor, gate_tiles),...  51.1 us
    pallas_call x1, Pallas kernels, core(): pl.pallas_call(core_kernel, name='core', out_shape=(jax.ShapeDtypeStruct(...  18.5 us
    unnamed x4, local copies, waits for them, and re-layouts  6.32 us

profile of v1, /device:TPU:1, one launch (start us, length us, event | category | flops | bytes accessed | tf_op | source)
XLA Modules:
  0.0 161.1 jit_solution(1273995994393899555)
XLA Ops:
  0.6 0.7 pad_bitcast_fusion
  1.3 1.3 select_maximum_fusion.small_ref
  2.6 1.3 reshape.38.conv_ref
  3.9 0.8 reshape.37
  4.7 1.6 %copy.20 = bf16[1,128,320]{2,1,0:T(8,128)(2,1)} copy(bf16[1,128,320]{1,2,0:T(8,128)(2,1)} %param.9) | data formatting | bytes 163840 | tf_op args[0]
  6.3 1.6 %copy.21 = bf16[1,128,320]{2,1,0:T(8,128)(2,1)} copy(bf16[1,128,320]{1,2,0:T(8,128)(2,1)} %param.17) | data formatting | bytes 163840 | tf_op args[8]
  8.0 1.7 %pad_maximum_fusion.w_ref = bf16[4,160,256]{2,1,0:T(8,128)(2,1)} fusion(bf16[1,160,256]{2,1,0:T(8,128)(2,1)} %bitcast.45, bf16[3,160,256]{2,1,0:T(8,128)(2,1)} %param.10), kind=kLoop, calls=%fused_computation | loop fusion | flops 163840 | bytes 655360 | tf_op jit(solution)/shard_map/concatenate | solution.py:601
  9.7 0.6 copy.22
  10.3 1.3 pad.15.wg_ref
  11.6 71.4 %gather.1 = (bf16[4,5120,256]{2,1,0:T(8,128)(2,1)}, bf16[16,128,320]{2,1,0:T(8,128)(2,1)}, bf16[16,128,320]{2,1,0:T(8,128)(2,1)}) custom-call(bf16[4,160,256]{2,1,0:T(8,128)(2,1)} %pad_maximum_fusion.w_ref, bf16[128,320]{1,0:T(8,128)(2,1)} %bitcast.41, bf16[128,320]{1,0:T(8,128)(2,1)} %bitcast.42), custom_call_target="tpu_custom_call" | custom-call | tf_op jit(solution)/shard_map/gather/pallas_call | solution.py:187
  83.0 18.5 %core.1 = (bf16[128,256]{1,0:T(8,128)(2,1)}, bf16[128,896]{1,0:T(8,128)(2,1)}, f32[32,8,128]{2,1,0:T(8,128)}, f32[8,128]{1,0:T(8,128)}) custom-call(bf16[4,5120,256]{2,1,0:T(8,128)(2,1)} %get-tuple-element.17.wf_ref, bf16[16,128,320]{2,1,0:T(8,128)(2,1)} %get-tuple-element.18.xf_ref, bf16[16,128,320]{2,1,0:T(8,128)(2,1)} %get-tuple-element.19.gf_ref, ...), custom_call_target="tpu_custom_call" | custom-call | tf_op jit(solution)/shard_map/core/pallas_call | solution.py:401
  101.5 51.1 %reduce.1 = (bf16[320,128]{1,0:T(8,128)(2,1)}, bf16[320,128]{1,0:T(8,128)(2,1)}, f32[32,8,128]{2,1,0:T(8,128)}) custom-call(bf16[4,5120,256]{2,1,0:T(8,128)(2,1)} %get-tuple-element.17.wf_ref, bf16[5120,128]{1,0:T(8,128)(2,1)} %pad.15.wg_ref, bf16[128,256]{1,0:T(8,128)(2,1)} %get-tuple-element.20.core_ref, bf16[128,896]{1,0:T(8,128)(2,1)} %get-tuple-element.21.low_ref, ...), custom_call_target="tpu_custom_call" | custom-call | tf_op jit(solution)/shard_map/reduce/pallas_call | solution.py:569
  152.6 1.2 slice_bitcast_fusion.1
  153.8 0.7 slice_bitcast_fusion
  154.5 0.5 slice_bitcast_fusion.2
  155.0 1.3 slice.25
  156.3 0.9 slice.23
  157.3 0.1 reshape.40
  157.3 0.8 reshape.41
  158.1 1.5 copy.29
  159.6 1.5 copy.30
  (1 shorter events, 0.0 us)

commit v2 on v0

v2 whole, which is shorter than its diff:
```python
import functools
import math

import jax
import jax.numpy as jnp
from jax import lax
from jax.experimental import pallas as pl
from jax.experimental.pallas import tpu as pltpu
from jax.sharding import PartitionSpec as P

MESH = pl.DeviceIdType.MESH
F32, BF16 = jnp.float32, jnp.bfloat16
LEN = 128
HEAD = 128
TAPS = 4
CORES = 2
ZL = 2
NN = (((1,), (0,)), ((), ()))
NT = (((1,), (1,)), ((), ()))


class Place:
    def __init__(self, dp, tensor):
        self.ny = dp // (ZL * CORES)
        self.nz = 4 if tensor == 16 else 2
        self.nx = tensor // self.nz
        d, t = lax.axis_index("dp"), lax.axis_index("tensor")
        self.d, self.t = d, t
        self.zl = d // (self.ny * CORES)
        self.y = (d // CORES) % self.ny
        self.c = d % CORES
        self.zh = t // self.nx
        self.x = t % self.nx

    def dp_of(self, zl, y, c):
        return zl * (self.ny * CORES) + y * CORES + c

    def at_y(self, step):
        return self.dp_of(self.zl, (self.y + step + self.ny) % self.ny, self.c), self.t

    def at_z(self):
        return self.dp_of(1 - self.zl, self.y, self.c), self.t

    def at_core(self):
        return self.dp_of(self.zl, self.y, 1 - self.c), self.t

    def at_zh(self, step):
        return self.d, ((self.zh + step + self.nz) % self.nz) * self.nx + self.x

    def at_x(self, step):
        return self.d, self.zh * self.nx + (self.x + step + self.nx) % self.nx


def remote(src, dst, send, recv, where):
    return pltpu.make_async_remote_copy(
        src_ref=src, dst_ref=dst, send_sem=send, recv_sem=recv, device_id=where, device_id_type=MESH
    )


def meet(peers):
    barrier = pltpu.get_barrier_semaphore()
    for where in peers:
        pl.semaphore_signal(barrier, inc=1, device_id=where, device_id_type=MESH)
    pl.semaphore_wait(barrier, len(peers))


def halves(a):
    high = a.astype(BF16)
    return high, (a - high.astype(F32)).astype(BF16)


def dot(a, b, dims=NN):
    return lax.dot_general(a, b, dims, preferred_element_type=F32)


def product(a, b, dims=NN):
    ah, al = halves(a)
    bh, bl = halves(b)
    side = 0 if dims is NN else 1
    return dot(jnp.concatenate([ah, ah, al], 1), jnp.concatenate([bh, bl, bh], side), dims)


def triangle_product(triangle, a):
    high = a.astype(BF16)
    rest = a - high.astype(F32)
    mid = rest.astype(BF16)
    low = (rest - mid.astype(F32)).astype(BF16)
    return dot(jnp.concatenate([triangle] * 3, 1), jnp.concatenate([high, mid, low], 0))


def unit_inverse(lower, xor):
    inverse = jnp.where(xor == 0, 1.0, 0.0) - jnp.where(xor == 1, lower, 0.0)
    width = 2
    while width < lower.shape[0]:
        between = jnp.where((xor >= width) & (xor < 2 * width), lower, 0.0)
        inverse = inverse - product(product(inverse, between), inverse)
        width *= 2
    return inverse


def head_forward(q, k, v, beta, c_col, c_row, within, strict, xor):
    fading = jnp.where(within, jnp.exp(jnp.where(within, c_col - c_row, 0.0)), 0.0)
    faded_keys = jnp.where(strict, fading * product(k, k, NT), 0.0)
    lower = beta * faded_keys
    inverse = unit_inverse(lower, xor)
    rows = product(inverse, beta * v)
    scores = fading * product(q, k, NT)
    return fading, faded_keys, lower, inverse, rows, scores, product(scores, rows)


def head_backward(q, k, v, beta, fading, faded_keys, lower, inverse, rows, scores, d_out, within, strict):
    d_scores = jnp.where(within, product(d_out, rows, NT), 0.0)
    d_rows = product(scores.T, d_out)
    d_target = product(inverse.T, d_rows)
    d_lower = jnp.where(strict, -product(d_target, rows, NT), 0.0)
    faded = fading * d_scores
    both = beta * fading * d_lower
    dq = product(faded, k)
    dk = product(faded.T, q) + product(both + both.T, k)
    dv = beta * d_target
    spread = d_scores * scores + d_lower * lower
    dc = jnp.sum(spread - spread.T, 1, keepdims=True)
    d_beta = jnp.sum(d_lower * faded_keys + d_target * v, 1, keepdims=True)
    return dq, dk, dv, dc, d_beta


def shifted(a, step, row):
    if step == 0:
        return a
    size = a.shape[0]
    moved = pltpu.roll(a, step % size, 0)
    keep = row >= step if step > 0 else row < size + step
    return jnp.where(keep, moved, 0.0)


class Stream:
    def __init__(self, here, early, mine, full, sems):
        self.here, self.early = here, early
        self.far = here.ny // 2
        self.shard = mine.shape[-2]
        self.half = self.shard // 2
        self.mine, self.full = mine, full
        self.yp, self.ym, self.z, self.c = (sems[i : i + 2] for i in (0, 2, 4, 6))
        self.sent = []

    def rows(self, ref, start, size):
        return ref.at[:, pl.ds(start, size), :] if len(ref.shape) == 3 else ref.at[pl.ds(start, size), :]

    def block(self, p, place, h, other_core=False):
        here = self.here
        zl = here.zl if p == 0 else 1 - here.zl
        c = 1 - here.c if other_core else here.c
        d = here.dp_of(zl, (here.y - place + here.ny) % here.ny, c)
        return self.rows(self.full, pl.multiple_of(d * self.shard + h * self.half, 16), self.half)

    def send(self, src, dst, sems, index, where):
        copy = remote(src, dst, sems[0].at[index], sems[1].at[index], where)
        copy.start()
        self.sent.append(copy)

    def arrive(self, dst, sems, index):
        remote(dst, dst, sems[0].at[index], sems[1].at[index], self.here.at_core()).wait_recv()

    def travels(self, direction, k, h):
        return k < self.far or (k == self.far and h == (0 if direction > 0 else 1))

    def along_y(self, src, dst, direction, k, p, h):
        if self.travels(direction, k, h):
            self.send(src, dst, self.yp if direction > 0 else self.ym, (k - 1, p, h), self.here.at_y(direction))

    def to_core(self, src, dst, p, place, h):
        self.send(src, dst, self.c, (p, place, h), self.here.at_core())

    def start(self):
        here = self.here
        for h in range(2):
            src, dst = self.rows(self.mine, h * self.half, self.half), self.block(0, 0, h)
            self.along_y(src, dst, 1, 1, 0, h)
            self.along_y(src, dst, -1, 1, 0, h)
            self.send(src, dst, self.z, (0, h), here.at_z())

    def own_to_core(self):
        for h in range(2):
            self.to_core(self.rows(self.mine, h * self.half, self.half), self.block(0, 0, h), 0, 0, h)

    def places(self, k):
        far, ny = self.far, self.here.ny
        return [k] if k in (0, far) else [k, ny - k]

    def from_z(self, k):
        for place in self.places(k):
            for h in range(2):
                got = self.block(1, place, h)
                self.arrive(got, self.z, (place, h))
                if self.early:
                    self.along_y(got, got, 1, 1, 1, h)
                    self.along_y(got, got, -1, 1, 1, h)
                self.to_core(got, got, 1, place, h)

    def from_y(self, k):
        here = self.here
        for p in range(2 if self.early else 1):
            for h in range(2):
                for direction in (1, -1):
                    if not self.travels(direction, k, h):
                        continue
                    place = k if direction > 0 else here.ny - k
                    got = self.block(p, place, h)
                    self.arrive(got, self.yp if direction > 0 else self.ym, (k - 1, p, h))
                    self.along_y(got, got, direction, k + 1, p, h)
                    if not self.early:
                        self.send(got, got, self.z, (place, h), here.at_z())
                    self.to_core(got, got, p, place, h)

    def from_core(self, k):
        for p in range(2):
            for place in self.places(k):
                for h in range(2):
                    self.arrive(self.block(p, place, h, True), self.c, (p, place, h))

    def finish(self):
        for copy in self.sent:
            copy.wait_send()


def stream_sems(ny, early):
    dma = pltpu.SemaphoreType.DMA
    sems = []
    for dims in ((ny // 2, 2 if early else 1, 2),) * 2 + ((1 if early else ny, 2), (2, ny, 2)):
        sems += [dma(dims), dma(dims)]
    return sems


def layer_kernel(
    dp, tensor, w_ref, wo_ref, x_ref, g_ref, wg_ref, conv_ref, rate_ref, bias_ref, gain_ref, res_ref, sum_ref, *scratch
):
    scratch = list(scratch)

    def take(n):
        out = scratch[:n]
        del scratch[:n]
        return out

    wf, wof, xt, gt, xr, gr, wg16, gcol, proj, back, core_low, low, pack = take(13)
    parts, r1, keep, r2, gx, gz, mine, ry, rz, fin, all_sums = take(11)
    own_sem, t1s, t1r, t2s, t2r, s1s, s1r, s2s, s2r, gxs, gxr, gzs, gzr, rys, ryr, rzs, rzr, ays, ayr = take(19)
    here = Place(dp, tensor)
    ny, nz, nx = here.ny, here.nz, here.nx
    far = ny // 2
    part = x_ref.shape[0]
    width = w_ref.shape[2]
    heads = width // HEAD
    each = pack.shape[0] // ny
    gate_tiles = xt.shape[0] // 256
    q = here.zl * CORES + here.c

    qk = Stream(here, True, w_ref.at[pl.ds(0, 2)], wf.at[pl.ds(0, 2)], take(8))
    vv = Stream(here, False, w_ref.at[2], wf.at[2], take(8))
    oo = Stream(here, False, wo_ref, wof, take(8))
    sent = []

    def at_q(r):
        other = q ^ r
        return here.dp_of(other // CORES, here.y, other % CORES), here.t

    def send(src, dst, s, r, where):
        copy = remote(src, dst, s, r, where)
        copy.start()
        sent.append(copy)

    def arrive(dst, s, r):
        remote(dst, dst, s, r, here.at_core()).wait_recv()

    def back_of(step, size, now):
        return (now - step + size) % size

    def slot(ref, t):
        return ref.at[pl.ds(pl.multiple_of(t * part, 16), part), :]

    meet(
        [here.at_y(s) for s in range(1, ny)]
        + [at_q(r) for r in range(1, 4)]
        + [here.at_zh(s) for s in range(1, nz)]
        + [here.at_x(s) for s in range(1, nx)]
    )

    arrays = ((x_ref, xt), (g_ref, gt))
    qk.start()
    vv.start()
    for a, (src, dst) in enumerate(arrays):
        for s in range(1, nz):
            send(src, slot(dst, here.t), t1s.at[s - 1, a], t1r.at[s - 1, a], here.at_zh(s))
        for s in range(1, nx):
            send(src, slot(dst, here.t), t2s.at[s - 1, 0, a], t2r.at[s - 1, 0, a], here.at_x(s))
    qk.own_to_core()
    vv.own_to_core()
    mine_rows = pl.ds(pl.multiple_of(here.d * w_ref.shape[1], 16), w_ref.shape[1])
    own = [
        pltpu.make_async_copy(x_ref, slot(xt, here.t), own_sem.at[0]),
        pltpu.make_async_copy(g_ref, slot(gt, here.t), own_sem.at[1]),
        pltpu.make_async_copy(w_ref, wf.at[:, mine_rows, :], own_sem.at[2]),
        pltpu.make_async_copy(wo_ref, wof.at[mine_rows, :], own_sem.at[3]),
    ]
    for copy in own:
        copy.start()

    proj[...] = jnp.zeros_like(proj)
    back[...] = jnp.zeros_like(back)
    pack[...] = jnp.zeros_like(pack)
    wide = wg_ref[...].astype(F32)
    wg16[...] = jnp.concatenate([wide[0], wide[1], jnp.zeros((16 - 2 * heads, wide.shape[2]), F32)], 0).astype(BF16)

    def column(i, _):
        at = pl.ds(pl.multiple_of(i * 128, 128), 128)
        tall = jnp.concatenate([wg16[:, at].astype(F32), jnp.zeros((112, 128), F32)], 0)
        gcol[at, :] = tall.T.astype(BF16)
        return 0

    lax.fori_loop(0, xt.shape[0] // 128, column, 0)
    qk.from_z(0)
    for copy in own:
        copy.wait()

    def spread():
        for a, (_, dst) in enumerate(arrays):
            for s in range(1, nz):
                got = slot(dst, back_of(s, nz, here.zh) * nx + here.x)
                arrive(got, t1s.at[s - 1, a], t1r.at[s - 1, a])
                for sx in range(1, nx):
                    send(got, got, t2s.at[sx - 1, s, a], t2r.at[sx - 1, s, a], here.at_x(sx))

    def landed(a, turned):
        dst = arrays[a][1]
        for s in range(nz):
            for sx in range(1, nx):
                got = slot(dst, back_of(s, nz, here.zh) * nx + back_of(sx, nx, here.x))
                arrive(got, t2s.at[sx - 1, s, a], t2r.at[sx - 1, s, a])

        def turn(t, _):
            turned[t] = dst[pl.ds(pl.multiple_of(t * part, 16), part), :].T
            return 0

        lax.fori_loop(0, tensor, turn, 0)

    def contract(k):
        qk.from_core(k)
        vv.from_core(k)
        ways = len(qk.places(k))

        def term(i, _):
            zl = jnp.where(i // ways == 0, here.zl, 1 - here.zl)
            step = jnp.where(i % ways == 0, k, ny - k)
            t = zl * ny + (here.y - step + ny) % ny
            rows = pl.ds(pl.multiple_of(t * part, 16), part)
            x = xr[t]
            for s in range(3):
                proj[:, s * width : (s + 1) * width] += dot(x, wf[s, rows, :])
            return 0

        lax.fori_loop(0, 2 * ways, term, 0)

    todo = []
    turned_x = turned_g = False
    for k in range(1, far + 1):
        if k == far:
            oo.start()
            oo.own_to_core()
        qk.from_y(k)
        vv.from_y(k)
        vv.from_z(k - 1)
        todo.append(k - 1)
        if k == 1:
            spread()
        if k >= 2:
            if not turned_x:
                landed(0, xr)
                turned_x = True
            for j in todo:
                contract(j)
            todo = []
        if k >= 3 and not turned_g:
            landed(1, gr)
            turned_g = True
    if not turned_x:
        landed(0, xr)
    logits_t = dot(wg16[...], xt[...])
    vv.from_z(far)
    for j in [*todo, far]:
        contract(j)
    if not turned_g:
        landed(1, gr)
    oo.from_y(1)
    oo.from_z(0)

    row = lax.broadcasted_iota(jnp.int32, (LEN, LEN), 0)
    lane = lax.broadcasted_iota(jnp.int32, (LEN, LEN), 1)
    wide_row = lax.broadcasted_iota(jnp.int32, (LEN, width), 0)
    within, strict, xor = row >= lane, row > lane, row ^ lane
    triangle = jnp.where(within, 1.0, 0.0).astype(BF16)
    triangle_t = jnp.where(row <= lane, 1.0, 0.0).astype(BF16)
    lane_1 = lax.broadcasted_iota(jnp.int32, (1, LEN), 1)
    rate = sum(jnp.where(lane_1 == h, rate_ref[h], 0.0) for h in range(heads))
    bias = sum(jnp.where(lane_1 == h, bias_ref[h], 0.0) for h in range(heads))
    gain = gain_ref[...]

    logits = jnp.concatenate([logits_t, jnp.zeros((LEN - 16, LEN), F32)], 0).T
    pre = logits + bias
    soft = jnp.maximum(pre, 0.0) + jnp.log1p(jnp.exp(-jnp.abs(pre)))
    strength = 1.0 / (1.0 + jnp.exp(-logits))
    cumulative = triangle_product(triangle, -rate * soft)
    cumulative_t = cumulative.T

    before, gate, active = [], [], []
    for s in range(3):
        p = proj[:, s * width : (s + 1) * width]
        z = jnp.zeros_like(p)
        for i in range(TAPS):
            z = z + conv_ref[s, i : i + 1, :] * shifted(p, TAPS - 1 - i, wide_row)
        sigma = 1.0 / (1.0 + jnp.exp(-z))
        before.append(z)
        gate.append(sigma)
        active.append(z * sigma)

    for k in range(2, far + 1):
        oo.from_y(k)
        oo.from_z(k - 1)

    scale = 1.0 / math.sqrt(HEAD)
    kept = []
    for h in range(heads):
        cut = slice(h * HEAD, (h + 1) * HEAD)
        aq, ak, v = active[0][:, cut], active[1][:, cut], active[2][:, cut]
        nq = lax.rsqrt(jnp.sum(aq * aq, 1, keepdims=True) + 1e-6)
        nk = lax.rsqrt(jnp.sum(ak * ak, 1, keepdims=True) + 1e-6)
        uq, k = aq * nq, ak * nk
        beta = strength[:, heads + h : heads + h + 1]
        held = head_forward(uq * scale, k, v, beta, cumulative[:, h : h + 1], cumulative_t[h : h + 1, :], within, strict, xor)
        out = held[-1]
        r = lax.rsqrt(jnp.mean(out * out, 1, keepdims=True) + 1e-5)
        normed = out * r
        core_low[:, cut] = (normed * gain).astype(BF16)
        kept.append((nq, nk, uq, k, v, beta, held[:-1], r, normed))

    oo.from_z(far)
    for k in range(far + 1):
        oo.from_core(k)

    def first(a, build):
        def piece(i, _):
            sx, zh = (i // nz + 1) % nx, i % nz
            x = (here.x + sx) % nx
            t = zh * nx + x
            parts[a, t] = build(pl.ds(pl.multiple_of(t * part, 16), part)).astype(BF16)

            @pl.when(sx != 0)
            def _():
                remote(parts.at[a, t], r1.at[a, sx, zh], s1s.at[a, sx, zh], s1r.at[a, sx, zh], (here.d, here.zh * nx + x)).start()

            return 0

        lax.fori_loop(0, nx * nz, piece, 0)

    def second(a):
        for sz in [*range(1, nz), 0]:
            zh = (here.zh + sz) % nz
            total = parts[a, zh * nx + here.x].astype(F32)
            for sx in range(1, nx):
                arrive(r1.at[a, sx, zh], s1s.at[a, sx, zh], s1r.at[a, sx, zh])
                total = total + r1[a, sx, zh].astype(F32)
            if sz:
                mine[a, sz] = total.astype(BF16)
                send(mine.at[a, sz], r2.at[a, sz], s2s.at[a, sz], s2r.at[a, sz], here.at_zh(sz))
            else:
                keep[a] = total

    def last(a):
        total = keep[a]
        for sz in range(1, nz):
            arrive(r2.at[a, sz], s2s.at[a, sz], s2r.at[a, sz])
            total = total + r2[a, sz].astype(F32)
        res_ref[a] = total.astype(BF16)

    first(0, lambda rows: dot(wof[rows, :], core_low[...], NT))

    def back_term(t, _):
        back[...] += dot(gr[t], wof[pl.ds(pl.multiple_of(t * part, 16), part), :])
        return 0

    lax.fori_loop(0, tensor, back_term, 0)

    gain_grad = jnp.zeros((1, HEAD), F32)
    for h in range(heads):
        gain_grad = gain_grad + jnp.sum(back[:, h * HEAD : (h + 1) * HEAD] * kept[h][-1], 0, keepdims=True)
    gx[here.x] = jnp.concatenate([gain_grad, jnp.zeros((7, HEAD), F32)], 0)
    for s in range(1, nx):
        send(gx.at[here.x], gx.at[here.x], gxs.at[s - 1], gxr.at[s - 1], here.at_x(s))

    d_active = [[None] * heads for _ in range(3)]
    dc_all = jnp.zeros((LEN, LEN), F32)
    db_all = jnp.zeros((LEN, LEN), F32)
    for h in range(heads):
        nq, nk, uq, k, v, beta, held, r, normed = kept[h]
        dn = back[:, h * HEAD : (h + 1) * HEAD] * gain
        d_out = r * (dn - normed * jnp.mean(dn * normed, 1, keepdims=True))
        dq, dk, dv, dc, d_beta = head_backward(uq * scale, k, v, beta, *held, d_out, within, strict)
        dq = dq * scale
        d_active[0][h] = nq * (dq - uq * jnp.sum(uq * dq, 1, keepdims=True))
        d_active[1][h] = nk * (dk - k * jnp.sum(k * dk, 1, keepdims=True))
        d_active[2][h] = dv
        dc_all = jnp.where(lane == h, dc, dc_all)
        db_all = jnp.where(lane == heads + h, d_beta, db_all)

    for s in range(1, nx):
        arrive(gx.at[back_of(s, nx, here.x)], gxs.at[s - 1], gxr.at[s - 1])
    gz[here.zh] = sum(gx[i] for i in range(nx))
    for s in range(1, nz):
        send(gz.at[here.zh], gz.at[here.zh], gzs.at[s - 1], gzr.at[s - 1], here.at_zh(s))

    d_decay = triangle_product(triangle_t, dc_all)
    d_pre = -rate * d_decay / (1.0 + jnp.exp(-pre))
    pack[gate_tiles + 3, 1:2, :] = jnp.sum(-soft * d_decay, 0, keepdims=True)
    pack[gate_tiles + 3, 2:3, :] = jnp.sum(d_pre, 0, keepdims=True)
    d_logits = (d_pre + db_all * strength * (1.0 - strength)).astype(BF16)
    low[:, 3 * width :] = d_logits
    d_logits_t = d_logits.astype(F32).T[0:16, :].astype(BF16)

    for s in range(3):
        z, sigma = before[s], gate[s]
        dz = jnp.concatenate(d_active[s], 1) * (sigma * (1.0 + z * (1.0 - sigma)))
        p = proj[:, s * width : (s + 1) * width]
        dp_s = jnp.zeros_like(p)
        for i in range(TAPS):
            ahead = shifted(dz, i + 1 - TAPS, wide_row)
            dp_s = dp_s + conv_ref[s, i : i + 1, :] * ahead
            total = jnp.sum(ahead * p, 0, keepdims=True)
            for j in range(width // 128):
                at = j * TAPS + i
                pack[gate_tiles + s, at : at + 1, :] = total[:, j * 128 : (j + 1) * 128]
        low[:, s * width : (s + 1) * width] = dp_s.astype(BF16)

    def grad_in(rows):
        total = dot(gcol[rows, :], low[:, 3 * width :], NT)
        for s in range(3):
            total = total + dot(wf[s, rows, :], low[:, s * width : (s + 1) * width], NT)
        return total

    first(1, grad_in)

    def gates(i, _):
        grad = dot(d_logits_t, xt[pl.ds(pl.multiple_of(i * 256, 256), 256), :], NT)
        pack[i, 0:4, :] = grad[0:4, 0:128]
        pack[i, 4:8, :] = grad[0:4, 128:256]
        return 0

    lax.fori_loop(0, gate_tiles, gates, 0)

    for s in range(1, nz):
        arrive(gz.at[back_of(s, nz, here.zh)], gzs.at[s - 1], gzr.at[s - 1])
    pack[gate_tiles + 3, 0:1, :] = sum(gz[i, 0:1, :] for i in range(nz))
    for s in range(1, ny):
        there = (here.y + s) % ny
        send(pack.at[pl.ds(there * each, each)], ry.at[here.y], rys.at[s - 1], ryr.at[s - 1], here.at_y(s))
    ry[here.y] = pack[pl.ds(here.y * each, each)]

    second(0)

    for s in range(1, ny):
        arrive(ry.at[back_of(s, ny, here.y)], rys.at[s - 1], ryr.at[s - 1])
    rz[q] = sum(ry[i] for i in range(ny))
    for r in range(1, 4):
        send(rz.at[q], rz.at[q], rzs.at[r - 1], rzr.at[r - 1], at_q(r))

    last(0)
    second(1)

    for r in range(1, 4):
        arrive(rz.at[q ^ r], rzs.at[r - 1], rzr.at[r - 1])
    fin[...] = sum(rz[i] for i in range(4))
    for s in range(1, ny):
        send(fin, all_sums.at[here.y], ays.at[s - 1], ayr.at[s - 1], here.at_y(s))
    all_sums[here.y] = fin[...]
    for s in range(1, ny):
        arrive(all_sums.at[back_of(s, ny, here.y)], ays.at[s - 1], ayr.at[s - 1])
    for i in range(ny):
        sum_ref[i * each : (i + 1) * each] = all_sums[i]

    last(1)

    def finished(i, _):
        sx, zh = i // nz + 1, i % nz
        for a in range(2):
            remote(parts.at[a, 0], r1.at[a, sx, zh], s1s.at[a, sx, zh], s1r.at[a, sx, zh], here.at_core()).wait_send()
        return 0

    lax.fori_loop(0, (nx - 1) * nz, finished, 0)
    for stream in (qk, vv, oo):
        stream.finish()
    for copy in sent:
        copy.wait_send()


def layer(dp, tensor, w, wo, x, g, wg, conv, rate, bias, gain):
    ny = dp // (ZL * CORES)
    nz = 4 if tensor == 16 else 2
    nx = tensor // nz
    part = x.shape[0]
    model, width = part * tensor, w.shape[2]
    tiles = pl.cdiv(model // 256 + 4, ny) * ny
    each = tiles // ny
    any_spec = pl.BlockSpec(memory_space=pl.ANY)
    vmem = pl.BlockSpec(memory_space=pltpu.VMEM)
    smem = pl.BlockSpec(memory_space=pltpu.SMEM)
    dma = pltpu.SemaphoreType.DMA
    sems = [dma((4,))]
    for dims in (
        (nz - 1, 2), (nx - 1, nz, 2), (2, nx, nz), (2, nz), (nx - 1,), (nz - 1,), (ny - 1,), (3,), (ny - 1,),
    ):
        sems += [dma(dims), dma(dims)]
    sems += stream_sems(ny, True) + stream_sems(ny, False) + stream_sems(ny, False)
    return pl.pallas_call(
        functools.partial(layer_kernel, dp, tensor),
        name="layer",
        out_shape=(jax.ShapeDtypeStruct((2, part, LEN), BF16), jax.ShapeDtypeStruct((tiles, 8, 128), F32)),
        in_specs=[any_spec] * 4 + [vmem] * 2 + [smem] * 2 + [vmem],
        out_specs=(vmem,) * 2,
        scratch_shapes=[
            pltpu.VMEM((3, model, width), BF16),
            pltpu.VMEM((model, width), BF16),
            pltpu.VMEM((model, LEN), BF16),
            pltpu.VMEM((model, LEN), BF16),
            pltpu.VMEM((tensor, LEN, part), BF16),
            pltpu.VMEM((tensor, LEN, part), BF16),
            pltpu.VMEM((16, model), BF16),
            pltpu.VMEM((model, 128), BF16),
            pltpu.VMEM((LEN, 3 * width), F32),
            pltpu.VMEM((LEN, width), F32),
            pltpu.VMEM((LEN, width), BF16),
            pltpu.VMEM((LEN, 3 * width + 128), BF16),
            pltpu.VMEM((tiles, 8, 128), F32),
            pltpu.VMEM((2, tensor, part, LEN), BF16),
            pltpu.VMEM((2, nx, nz, part, LEN), BF16),
            pltpu.VMEM((2, part, LEN), F32),
            pltpu.VMEM((2, nz, part, LEN), BF16),
            pltpu.VMEM((nx, 8, 128), F32),
            pltpu.VMEM((nz, 8, 128), F32),
            pltpu.VMEM((2, nz, part, LEN), BF16),
            pltpu.VMEM((ny, each, 8, 128), F32),
            pltpu.VMEM((4, each, 8, 128), F32),
            pltpu.VMEM((each, 8, 128), F32),
            pltpu.VMEM((ny, each, 8, 128), F32),
        ]
        + sems,
        compiler_params=pltpu.CompilerParams(collective_id=0, has_side_effects=True, vmem_limit_bytes=56 * 2**20),
    )(w, wo, x, g, wg, conv, rate, bias, gain)


def split_kernel(res_ref, sum_ref, out_ref, gin_ref, gates_ref, conv_ref, rate_ref, bias_ref, gain_ref):
    out_ref[...] = res_ref[0]
    gin_ref[...] = res_ref[1]
    heads = gates_ref.shape[1]
    count = gates_ref.shape[2] // 256
    for i in range(count):
        for j in range(2):
            for s in range(2):
                at = j * 4 + s * heads
                gates_ref[s, :, i * 256 + j * 128 : i * 256 + (j + 1) * 128] = sum_ref[i, at : at + heads, :]
    for s in range(3):
        for j in range(2):
            conv_ref[s, :, j * 128 : (j + 1) * 128] = sum_ref[count + s, j * 4 : j * 4 + 4, :]
    rest = sum_ref[count + 3]
    row = lax.broadcasted_iota(jnp.int32, rest.shape, 0)
    lane = lax.broadcasted_iota(jnp.int32, rest.shape, 1)
    for h in range(heads):
        rate_ref[h] = jnp.sum(jnp.where((row == 1) & (lane == h), rest, 0.0))
        bias_ref[h] = jnp.sum(jnp.where((row == 2) & (lane == h), rest, 0.0))
    gain_ref[...] = rest[0:1, :]


def on_device(dp, tensor, inputs, w_qkv, w_gates, conv_weight, decay_rate, gate_bias, norm_gain, w_out, grad_out):
    part, model = inputs.shape[2], w_gates.shape[1]
    heads, width = decay_rate.shape[0], w_qkv.shape[2]
    res, total = layer(
        dp, tensor, w_qkv, w_out.T, inputs[0].T, grad_out[0].T, w_gates.transpose(0, 2, 1), conv_weight,
        decay_rate, gate_bias, norm_gain[None],
    )
    vmem = pl.BlockSpec(memory_space=pltpu.VMEM)
    smem = pl.BlockSpec(memory_space=pltpu.SMEM)
    out, grad_in, gates, conv, rate, bias, gain = pl.pallas_call(
        split_kernel,
        name="split",
        out_shape=(
            jax.ShapeDtypeStruct((part, LEN), BF16),
            jax.ShapeDtypeStruct((part, LEN), BF16),
            jax.ShapeDtypeStruct((2, heads, model), F32),
            jax.ShapeDtypeStruct((3, TAPS, width), F32),
            jax.ShapeDtypeStruct((heads,), F32),
            jax.ShapeDtypeStruct((heads,), F32),
            jax.ShapeDtypeStruct((1, HEAD), F32),
        ),
        in_specs=[vmem] * 2,
        out_specs=(vmem,) * 4 + (smem,) * 2 + (vmem,),
    )(res, total)
    return (out.T[None], grad_in.T[None], gates.transpose(0, 2, 1), conv, rate, bias, gain[0])


def solution(mesh):
    dp, tensor = mesh.shape["dp"], mesh.shape["tensor"]
    return jax.shard_map(
        functools.partial(on_device, dp, tensor),
        mesh=mesh,
        in_specs=(
            P("dp", None, "tensor"),
            P(None, "dp", "tensor"),
            P(None, None, "tensor"),
            P(None, None, "tensor"),
            P("tensor"),
            P("tensor"),
            P(),
            P("tensor", "dp"),
            P("dp", None, "tensor"),
        ),
        out_specs=(
            P("dp", None, "tensor"),
            P("dp", None, "tensor"),
            P(None, None, "tensor"),
            P(None, None, "tensor"),
            P("tensor"),
            P("tensor"),
            P(),
        ),
        check_vma=False,
    )
```

time: 767 us -> 132 us (0.17)
  waiting for transfers between devices: 365 us -> 0 us
  blocking collectives: 205 us -> 0 us
  Pallas kernels: 0 us -> 131 us
  other arithmetic: 83.8 us -> 0 us
  matrix products: 53.8 us -> 0 us
  local copies, waits for them, and re-layouts: 41.6 us -> 0 us
  between operations: 14.9 us -> 0.64 us
    all_gather x4 -> x0, waiting for transfers between devices: 263 us -> none  [the longest x1 72.8 us: on_device(): lax.all_gather(w_qkv, 'dp', axis=1, tiled=True)]
    psum x2 -> x0, blocking collectives: 205 us -> none  [the longest x1 103 us: on_device(): lax.psum((gate_grad, conv_grad, rate_grad, bias_grad), 'dp')]
    pallas_call x0 -> x2, Pallas kernels: none -> 131 us  [the longest x1 130 us: layer(): pl.pallas_call(functools.partial(layer_kernel, dp, tensor), name='layer',...]
    psum x1 -> x0, waiting for transfers between devices: 99.5 us -> none  [on_device(): lax.psum((gate_grad, conv_grad, rate_grad, bias_grad), 'dp')]
    another operation x46 -> x0, other arithmetic: 48.3 us -> none  [the longest x20 45.3 us: advance(): jax.scipy.linalg.solve_triangular(system, target, lower=True, unit_diagon...]
    dot_general x45 -> x0, matrix products: 47 us -> none  [the longest x6 6.54 us: advance(): jnp.dot((update_rows * remain).T, key_part, precision=HI)]
    dynamic_update_slice x12 -> x0, other arithmetic: 11.9 us -> none  [head_scan(): lax.scan(advance, initial, (to_blocks(queries), to_blocks(key_rows), to_b...]
    unnamed x85 -> x0, local copies, waits for them, and re-layouts: 11.3 us -> none
  transfers between devices with their start and end apart: 7 -> 0, of which waited for: 5 -> 0; matrix products, arithmetic and copies ran while one was open for 12% -> 0% of each run, Pallas kernels for 0% -> 0%
where the time goes in v2:
time: 132 us
  Pallas kernels  131 us (99%)
    pallas_call x1, Pallas kernels, layer(): pl.pallas_call(functools.partial(layer_kernel, dp, tensor), name='layer',...  130 us

profile of v2, /device:TPU:1, one launch (start us, length us, event | category | flops | bytes accessed | tf_op | source)
XLA Modules:
  0.0 132.1 jit_solution(10057847712330254379)
XLA Ops:
  0.6 129.8 %layer.1 = (bf16[2,320,128]{2,1,0:T(8,128)(2,1)}, f32[24,8,128]{2,1,0:T(8,128)}) custom-call(bf16[3,160,256]{2,1,0:T(8,128)(2,1)} %w_ref.1, bf16[160,256]{1,0:T(8,128)(2,1)} %bitcast.17, bf16[320,128]{1,0:T(8,128)(2,1)} %bitcast.18, bf16[320,128]{1,0:T(8,128)(2,1)} %bitcast.19, bf16[2,2,5120]{2,1,0:T(2,128)(2,1)} %bitcast.20, f32[3,4,256]{2,1,0:T(4,128)} %conv_ref.1, ...), custom_call_target="tpu_custom_call" | custom-call | tf_op jit(solution)/shard_map/layer/pallas_call | solution.py:620
  130.4 1.7 %split.1 = (bf16[320,128]{1,0:T(8,128)(2,1)}, bf16[320,128]{1,0:T(8,128)(2,1)}, f32[2,2,5120]{2,1,0:T(2,128)}, f32[3,4,256]{2,1,0:T(4,128)}, f32[2]{0:T(128)}, /*index=5*/f32[2]{0:T(128)}, f32[1,128]{1,0:T(1,128)}) custom-call(bf16[2,320,128]{2,1,0:T(8,128)(2,1)} %get-tuple-element.16.res_ref, f32[24,8,128]{2,1,0:T(8,128)} %get-tuple-element.17.sum_ref), custom_call_target="tpu_custom_call" | custom-call | tf_op jit(solution)/shard_map/split/pallas_call | solution.py:688

commit v3 on v2

--- a/solution.py
+++ b/solution.py
@@ -15,6 +15,7 @@
 TAPS = 4
 CORES = 2
 ZL = 2
+EARLY = 2
 NN = (((1,), (0,)), ((), ()))
 NT = (((1,), (1,)), ((), ()))
 
@@ -134,83 +135,80 @@
 
 
 class Stream:
-    def __init__(self, here, early, mine, full, sems):
-        self.here, self.early = here, early
+    def __init__(self, here, early, full, shard, sems):
+        self.here, self.early, self.full = here, early, full
         self.far = here.ny // 2
-        self.shard = mine.shape[-2]
-        self.half = self.shard // 2
-        self.mine, self.full = mine, full
+        self.shard, self.half = shard, shard // 2
         self.yp, self.ym, self.z, self.c = (sems[i : i + 2] for i in (0, 2, 4, 6))
         self.sent = []
-
-    def rows(self, ref, start, size):
-        return ref.at[:, pl.ds(start, size), :] if len(ref.shape) == 3 else ref.at[pl.ds(start, size), :]
 
     def block(self, p, place, h, other_core=False):
         here = self.here
         zl = here.zl if p == 0 else 1 - here.zl
         c = 1 - here.c if other_core else here.c
         d = here.dp_of(zl, (here.y - place + here.ny) % here.ny, c)
-        return self.rows(self.full, pl.multiple_of(d * self.shard + h * self.half, 16), self.half)
-
-    def send(self, src, dst, sems, index, where):
-        copy = remote(src, dst, sems[0].at[index], sems[1].at[index], where)
+        return self.full.at[:, pl.ds(pl.multiple_of(d * self.shard + h * self.half, 16), self.half), :]
+
+    def send(self, ref, sems, index, where):
+        copy = remote(ref, ref, sems[0].at[index], sems[1].at[index], where)
         copy.start()
         self.sent.append(copy)
 
-    def arrive(self, dst, sems, index):
-        remote(dst, dst, sems[0].at[index], sems[1].at[index], self.here.at_core()).wait_recv()
+    def arrive(self, ref, sems, index):
+        remote(ref, ref, sems[0].at[index], sems[1].at[index], self.here.at_core()).wait_recv()
 
     def travels(self, direction, k, h):
         return k < self.far or (k == self.far and h == (0 if direction > 0 else 1))
 
-    def along_y(self, src, dst, direction, k, p, h):
+    def along_y(self, ref, direction, k, p, h):
         if self.travels(direction, k, h):
-            self.send(src, dst, self.yp if direction > 0 else self.ym, (k - 1, p, h), self.here.at_y(direction))
-
-    def to_core(self, src, dst, p, place, h):
-        self.send(src, dst, self.c, (p, place, h), self.here.at_core())
+            self.send(ref, self.yp if direction > 0 else self.ym, (k - 1, p, h), self.here.at_y(direction))
+
+    def along_z(self, ref, place, h):
+        self.send(ref, self.z, (place, h), self.here.at_z())
+
+    def to_core(self, ref, p, place, h):
+        self.send(ref, self.c, (p, place, h), self.here.at_core())
 
     def start(self):
-        here = self.here
         for h in range(2):
-            src, dst = self.rows(self.mine, h * self.half, self.half), self.block(0, 0, h)
-            self.along_y(src, dst, 1, 1, 0, h)
-            self.along_y(src, dst, -1, 1, 0, h)
-            self.send(src, dst, self.z, (0, h), here.at_z())
+            own = self.block(0, 0, h)
+            self.along_y(own, 1, 1, 0, h)
+            self.along_y(own, -1, 1, 0, h)
+            self.along_z(own, 0, h)
 
     def own_to_core(self):
         for h in range(2):
-            self.to_core(self.rows(self.mine, h * self.half, self.half), self.block(0, 0, h), 0, 0, h)
+            self.to_core(self.block(0, 0, h), 0, 0, h)
 
     def places(self, k):
-        far, ny = self.far, self.here.ny
-        return [k] if k in (0, far) else [k, ny - k]
+        return [k] if k in (0, self.far) else [k, self.here.ny - k]
 
     def from_z(self, k):
+        if self.early and k:
+            return
         for place in self.places(k):
             for h in range(2):
                 got = self.block(1, place, h)
                 self.arrive(got, self.z, (place, h))
                 if self.early:
-                    self.along_y(got, got, 1, 1, 1, h)
-                    self.along_y(got, got, -1, 1, 1, h)
-                self.to_core(got, got, 1, place, h)
+                    self.along_y(got, 1, 1, 1, h)
+                    self.along_y(got, -1, 1, 1, h)
+                self.to_core(got, 1, place, h)
 
     def from_y(self, k):
-        here = self.here
         for p in range(2 if self.early else 1):
             for h in range(2):
                 for direction in (1, -1):
                     if not self.travels(direction, k, h):
                         continue
-                    place = k if direction > 0 else here.ny - k
+                    place = k if direction > 0 else self.here.ny - k
                     got = self.block(p, place, h)
                     self.arrive(got, self.yp if direction > 0 else self.ym, (k - 1, p, h))
-                    self.along_y(got, got, direction, k + 1, p, h)
+                    self.along_y(got, direction, k + 1, p, h)
                     if not self.early:
-                        self.send(got, got, self.z, (place, h), here.at_z())
-                    self.to_core(got, got, p, place, h)
+                        self.along_z(got, place, h)
+                    self.to_core(got, p, place, h)
 
     def from_core(self, k):
         for p in range(2):
@@ -241,9 +239,9 @@
         del scratch[:n]
         return out
 
-    wf, wof, xt, gt, xr, gr, wg16, gcol, proj, back, core_low, low, pack = take(13)
-    parts, r1, keep, r2, gx, gz, mine, ry, rz, fin, all_sums = take(11)
-    own_sem, t1s, t1r, t2s, t2r, s1s, s1r, s2s, s2r, gxs, gxr, gzs, gzr, rys, ryr, rzs, rzr, ays, ayr = take(19)
+    wf, xt, gt, xr, gr, wg16, gcol, proj, back, core_low, low, pack = take(12)
+    parts, r1, relay, keep, r2, gx, gz, mine, ry, rz, fin, all_sums = take(12)
+    own_sem, t1s, t1r, t2s, t2r, s0s, s0r, s1s, s1r, s2s, s2r, gxs, gxr, gzs, gzr, rys, ryr, rzs, rzr, ays, ayr = take(21)
     here = Place(dp, tensor)
     ny, nz, nx = here.ny, here.nz, here.nx
     far = ny // 2
@@ -254,9 +252,9 @@
     gate_tiles = xt.shape[0] // 256
     q = here.zl * CORES + here.c
 
-    qk = Stream(here, True, w_ref.at[pl.ds(0, 2)], wf.at[pl.ds(0, 2)], take(8))
-    vv = Stream(here, False, w_ref.at[2], wf.at[2], take(8))
-    oo = Stream(here, False, wo_ref, wof, take(8))
+    shard = w_ref.shape[1]
+    early = Stream(here, True, wf.at[pl.ds(0, EARLY)], shard, take(8))
+    late = Stream(here, False, wf.at[pl.ds(EARLY, 4 - EARLY)], shard, take(8))
     sent = []
 
     def at_q(r):
@@ -277,6 +275,15 @@
     def slot(ref, t):
         return ref.at[pl.ds(pl.multiple_of(t * part, 16), part), :]
 
+    mine_rows = pl.ds(pl.multiple_of(here.d * shard, 16), shard)
+    own = [
+        pltpu.make_async_copy(w_ref, wf.at[pl.ds(0, 3), mine_rows, :], own_sem.at[0]),
+        pltpu.make_async_copy(wo_ref, wf.at[3, mine_rows, :], own_sem.at[1]),
+        pltpu.make_async_copy(x_ref, slot(xt, here.t), own_sem.at[2]),
+        pltpu.make_async_copy(g_ref, slot(gt, here.t), own_sem.at[3]),
+    ]
+    for copy in own:
+        copy.start()
     meet(
         [here.at_y(s) for s in range(1, ny)]
         + [at_q(r) for r in range(1, 4)]
@@ -284,25 +291,23 @@
         + [here.at_x(s) for s in range(1, nx)]
     )
 
-    arrays = ((x_ref, xt), (g_ref, gt))
-    qk.start()
-    vv.start()
-    for a, (src, dst) in enumerate(arrays):
-        for s in range(1, nz):
-            send(src, slot(dst, here.t), t1s.at[s - 1, a], t1r.at[s - 1, a], here.at_zh(s))
+    arrays = (xt, gt)
+
+    def set_out(a):
+        got = slot(arrays[a], here.t)
+        for s in sorted({1, nz - 1}):
+            send(got, got, t1s.at[s - 1, a], t1r.at[s - 1, a], here.at_zh(s))
         for s in range(1, nx):
-            send(src, slot(dst, here.t), t2s.at[s - 1, 0, a], t2r.at[s - 1, 0, a], here.at_x(s))
-    qk.own_to_core()
-    vv.own_to_core()
-    mine_rows = pl.ds(pl.multiple_of(here.d * w_ref.shape[1], 16), w_ref.shape[1])
-    own = [
-        pltpu.make_async_copy(x_ref, slot(xt, here.t), own_sem.at[0]),
-        pltpu.make_async_copy(g_ref, slot(gt, here.t), own_sem.at[1]),
-        pltpu.make_async_copy(w_ref, wf.at[:, mine_rows, :], own_sem.at[2]),
-        pltpu.make_async_copy(wo_ref, wof.at[mine_rows, :], own_sem.at[3]),
-    ]
+            send(got, got, t2s.at[s - 1, 0, a], t2r.at[s - 1, 0, a], here.at_x(s))
+
     for copy in own:
-        copy.start()
+        copy.wait()
+    late.start()
+    early.start()
+    set_out(0)
+    late.own_to_core()
+    early.own_to_core()
+    early.from_z(0)
 
     proj[...] = jnp.zeros_like(proj)
     back[...] = jnp.zeros_like(back)
@@ -317,20 +322,20 @@
         return 0
 
     lax.fori_loop(0, xt.shape[0] // 128, column, 0)
-    qk.from_z(0)
-    for copy in own:
-        copy.wait()
-
-    def spread():
-        for a, (_, dst) in enumerate(arrays):
-            for s in range(1, nz):
-                got = slot(dst, back_of(s, nz, here.zh) * nx + here.x)
-                arrive(got, t1s.at[s - 1, a], t1r.at[s - 1, a])
-                for sx in range(1, nx):
-                    send(got, got, t2s.at[sx - 1, s, a], t2r.at[sx - 1, s, a], here.at_x(sx))
+
+    def spread(a, steps):
+        for s in steps:
+            got = slot(arrays[a], back_of(s, nz, here.zh) * nx + here.x)
+            arrive(got, t1s.at[s - 1, a], t1r.at[s - 1, a])
+            if nz == 4 and s == (1 if a == 0 else 3):
+                send(got, got, t1s.at[1, a], t1r.at[1, a], here.at_zh(1 if a == 0 else -1))
+            for sx in range(1, nx):
+                send(got, got, t2s.at[sx - 1, s, a], t2r.at[sx - 1, s, a], here.at_x(sx))
+
+    near, further = sorted({1, nz - 1}), [2] if nz == 4 else []
 
     def landed(a, turned):
-        dst = arrays[a][1]
+        dst = arrays[a]
         for s in range(nz):
             for sx in range(1, nx):
                 got = slot(dst, back_of(s, nz, here.zh) * nx + back_of(sx, nx, here.x))
@@ -343,9 +348,9 @@
         lax.fori_loop(0, tensor, turn, 0)
 
     def contract(k):
-        qk.from_core(k)
-        vv.from_core(k)
-        ways = len(qk.places(k))
+        early.from_core(k)
+        late.from_core(k)
+        ways = len(early.places(k))
 
         def term(i, _):
             zl = jnp.where(i // ways == 0, here.zl, 1 - here.zl)
@@ -359,38 +364,37 @@
 
         lax.fori_loop(0, 2 * ways, term, 0)
 
-    todo = []
-    turned_x = turned_g = False
     for k in range(1, far + 1):
-        if k == far:
-            oo.start()
-            oo.own_to_core()
-        qk.from_y(k)
-        vv.from_y(k)
-        vv.from_z(k - 1)
-        todo.append(k - 1)
+        deep = k == far and far > 2
+        if deep:
+            landed(0, xr)
+            for j in range(far - 1):
+                contract(j)
+        late.from_y(k)
+        if deep:
+            late.from_z(k - 1)
+            landed(1, gr)
+            logits_t = dot(wg16[...], xt[...])
+        early.from_y(k)
+        if not deep:
+            late.from_z(k - 1)
         if k == 1:
-            spread()
-        if k >= 2:
-            if not turned_x:
-                landed(0, xr)
-                turned_x = True
-            for j in todo:
-                contract(j)
-            todo = []
-        if k >= 3 and not turned_g:
-            landed(1, gr)
-            turned_g = True
-    if not turned_x:
+            spread(0, near)
+            set_out(1)
+        if k == min(2, far):
+            spread(0, further)
+            spread(1, near)
+        if k == min(3, far):
+            spread(1, further)
+    late.from_z(far)
+    if far <= 2:
         landed(0, xr)
-    logits_t = dot(wg16[...], xt[...])
-    vv.from_z(far)
-    for j in [*todo, far]:
-        contract(j)
-    if not turned_g:
         landed(1, gr)
-    oo.from_y(1)
-    oo.from_z(0)
+        logits_t = dot(wg16[...], xt[...])
+        for j in range(far - 1):
+            contract(j)
+    contract(far - 1)
+    contract(far)
 
     row = lax.broadcasted_iota(jnp.int32, (LEN, LEN), 0)
     lane = lax.broadcasted_iota(jnp.int32, (LEN, LEN), 1)
@@ -420,10 +424,6 @@
         before.append(z)
         gate.append(sigma)
         active.append(z * sigma)
-
-    for k in range(2, far + 1):
-        oo.from_y(k)
-        oo.from_z(k - 1)
 
     scale = 1.0 / math.sqrt(HEAD)
     kept = []
@@ -441,32 +441,59 @@
         core_low[:, cut] = (normed * gain).astype(BF16)
         kept.append((nq, nk, uq, k, v, beta, held[:-1], r, normed))
 
-    oo.from_z(far)
-    for k in range(far + 1):
-        oo.from_core(k)
-
-    def first(a, build):
-        def piece(i, _):
-            sx, zh = (i // nz + 1) % nx, i % nz
-            x = (here.x + sx) % nx
-            t = zh * nx + x
+    part_half = part // 2
+    ends = [slice(0, part_half), slice(part_half, part)]
+    opposite = nx == 4
+    ways = [1, -1] if opposite else [1]
+
+    def along_x(a, sz, t, side, h):
+        rows = pl.ds(h * part_half, part_half)
+        return remote(
+            parts.at[a, t, rows], r1.at[a, side, sz, rows], s1s.at[a, side, sz, h], s1r.at[a, side, sz, h], here.at_x(ways[side])
+        )
+
+    def across(a, sz, t, h):
+        rows = pl.ds(h * part_half, part_half)
+        return remote(parts.at[a, t, rows], relay.at[a, sz, h], s0s.at[a, sz, h], s0r.at[a, sz, h], here.at_x(ways[h]))
+
+    def owner(sz, sx):
+        return ((here.zh + sz) % nz) * nx + (here.x + sx + nx) % nx
+
+    def pass_on(a, sz):
+        for h, way in enumerate(ways if opposite else []):
+            t = owner(sz, way)
+            across(a, sz, t, h).wait_recv()
+            parts[a, t, ends[h], :] = (parts[a, t, ends[h], :].astype(F32) + relay[a, sz, h].astype(F32)).astype(BF16)
+            along_x(a, sz, t, h, h).start()
+
+    def make(a, sz, build):
+        for sx in [2, *ways, 0] if opposite else [*ways, 0]:
+            t = owner(sz, sx)
             parts[a, t] = build(pl.ds(pl.multiple_of(t * part, 16), part)).astype(BF16)
 
-            @pl.when(sx != 0)
-            def _():
-                remote(parts.at[a, t], r1.at[a, sx, zh], s1s.at[a, sx, zh], s1r.at[a, sx, zh], (here.d, here.zh * nx + x)).start()
-
+    def ship(a, sz):
+        if opposite:
+            for h in range(2):
+                across(a, sz, owner(sz, 2), h).start()
+        for side, way in enumerate(ways):
+            for h in range(2):
+                if not opposite or h != side:
+                    along_x(a, sz, owner(sz, way), side, h).start()
+
+    def each_away(body):
+        def step(sz, _):
+            body(sz)
             return 0
 
-        lax.fori_loop(0, nx * nz, piece, 0)
-
-    def second(a):
-        for sz in [*range(1, nz), 0]:
-            zh = (here.zh + sz) % nz
-            total = parts[a, zh * nx + here.x].astype(F32)
-            for sx in range(1, nx):
-                arrive(r1.at[a, sx, zh], s1s.at[a, sx, zh], s1r.at[a, sx, zh])
-                total = total + r1[a, sx, zh].astype(F32)
+        lax.fori_loop(1, nz, step, 0)
+
+    def second(a, steps):
+        for sz in steps:
+            total = parts[a, owner(sz, 0)].astype(F32)
+            for side in range(len(ways)):
+                for h in range(2):
+                    along_x(a, sz, 0, side, h).wait_recv()
+                total = total + r1[a, side, sz].astype(F32)
             if sz:
                 mine[a, sz] = total.astype(BF16)
                 send(mine.at[a, sz], r2.at[a, sz], s2s.at[a, sz], s2r.at[a, sz], here.at_zh(sz))
@@ -480,13 +507,22 @@
             total = total + r2[a, sz].astype(F32)
         res_ref[a] = total.astype(BF16)
 
-    first(0, lambda rows: dot(wof[rows, :], core_low[...], NT))
+    def out_part(rows):
+        return dot(wf[3, rows, :], core_low[...], NT)
+
+    def out_step(sz):
+        make(0, sz, out_part)
+        ship(0, sz)
+
+    each_away(out_step)
 
     def back_term(t, _):
-        back[...] += dot(gr[t], wof[pl.ds(pl.multiple_of(t * part, 16), part), :])
+        back[...] += dot(gr[t], wf[3, pl.ds(pl.multiple_of(t * part, 16), part), :])
         return 0
 
     lax.fori_loop(0, tensor, back_term, 0)
+    make(0, 0, out_part)
+    each_away(lambda sz: pass_on(0, sz))
 
     gain_grad = jnp.zeros((1, HEAD), F32)
     for h in range(heads):
@@ -544,7 +580,12 @@
             total = total + dot(wf[s, rows, :], low[:, s * width : (s + 1) * width], NT)
         return total
 
-    first(1, grad_in)
+    def grad_step(sz):
+        make(1, sz, grad_in)
+        ship(1, sz)
+
+    each_away(grad_step)
+    make(1, 0, grad_in)
 
     def gates(i, _):
         grad = dot(d_logits_t, xt[pl.ds(pl.multiple_of(i * 256, 256), 256), :], NT)
@@ -562,7 +603,11 @@
         send(pack.at[pl.ds(there * each, each)], ry.at[here.y], rys.at[s - 1], ryr.at[s - 1], here.at_y(s))
     ry[here.y] = pack[pl.ds(here.y * each, each)]
 
-    second(0)
+    away = range(1, nz)
+    second(0, away)
+    each_away(lambda sz: pass_on(1, sz))
+    ship(1, 0)
+    ship(0, 0)
 
     for s in range(1, ny):
         arrive(ry.at[back_of(s, ny, here.y)], rys.at[s - 1], ryr.at[s - 1])
@@ -570,8 +615,9 @@
     for r in range(1, 4):
         send(rz.at[q], rz.at[q], rzs.at[r - 1], rzr.at[r - 1], at_q(r))
 
-    last(0)
-    second(1)
+    second(1, away)
+    pass_on(1, 0)
+    pass_on(0, 0)
 
     for r in range(1, 4):
         arrive(rz.at[q ^ r], rzs.at[r - 1], rzr.at[r - 1])
@@ -579,6 +625,11 @@
     for s in range(1, ny):
         send(fin, all_sums.at[here.y], ays.at[s - 1], ayr.at[s - 1], here.at_y(s))
     all_sums[here.y] = fin[...]
+
+    second(1, [0])
+    second(0, [0])
+    last(0)
+
     for s in range(1, ny):
         arrive(all_sums.at[back_of(s, ny, here.y)], ays.at[s - 1], ayr.at[s - 1])
     for i in range(ny):
@@ -586,15 +637,18 @@
 
     last(1)
 
-    def finished(i, _):
-        sx, zh = i // nz + 1, i % nz
+    def finished(sz, _):
         for a in range(2):
-            remote(parts.at[a, 0], r1.at[a, sx, zh], s1s.at[a, sx, zh], s1r.at[a, sx, zh], here.at_core()).wait_send()
+            for h in range(2):
+                for side in range(len(ways)):
+                    along_x(a, sz, 0, side, h).wait_send()
+                if opposite:
+                    across(a, sz, 0, h).wait_send()
         return 0
 
-    lax.fori_loop(0, (nx - 1) * nz, finished, 0)
-    for stream in (qk, vv, oo):
-        stream.finish()
+    lax.fori_loop(0, nz, finished, 0)
+    early.finish()
+    late.finish()
     for copy in sent:
         copy.wait_send()
 
@@ -613,10 +667,10 @@
     dma = pltpu.SemaphoreType.DMA
     sems = [dma((4,))]
     for dims in (
-        (nz - 1, 2), (nx - 1, nz, 2), (2, nx, nz), (2, nz), (nx - 1,), (nz - 1,), (ny - 1,), (3,), (ny - 1,),
+        (nz - 1, 2), (nx - 1, nz, 2), (2, nz, 2), (2, 2, nz, 2), (2, nz), (nx - 1,), (nz - 1,), (ny - 1,), (3,), (ny - 1,),
     ):
         sems += [dma(dims), dma(dims)]
-    sems += stream_sems(ny, True) + stream_sems(ny, False) + stream_sems(ny, False)
+    sems += stream_sems(ny, True) + stream_sems(ny, False)
     return pl.pallas_call(
         functools.partial(layer_kernel, dp, tensor),
         name="layer",
@@ -624,8 +678,7 @@
         in_specs=[any_spec] * 4 + [vmem] * 2 + [smem] * 2 + [vmem],
         out_specs=(vmem,) * 2,
         scratch_shapes=[
-            pltpu.VMEM((3, model, width), BF16),
-            pltpu.VMEM((model, width), BF16),
+            pltpu.VMEM((4, model, width), BF16),
             pltpu.VMEM((model, LEN), BF16),
             pltpu.VMEM((model, LEN), BF16),
             pltpu.VMEM((tensor, LEN, part), BF16),
@@ -638,7 +691,8 @@
             pltpu.VMEM((LEN, 3 * width + 128), BF16),
             pltpu.VMEM((tiles, 8, 128), F32),
             pltpu.VMEM((2, tensor, part, LEN), BF16),
-            pltpu.VMEM((2, nx, nz, part, LEN), BF16),
+            pltpu.VMEM((2, 2, nz, part, LEN), BF16),
+            pltpu.VMEM((2, nz, 2, part // 2, LEN), BF16),
             pltpu.VMEM((2, part, LEN), F32),
             pltpu.VMEM((2, nz, part, LEN), BF16),
             pltpu.VMEM((nx, 8, 128), F32),

time: 132 us -> 111 us (0.84)
  Pallas kernels: 131 us -> 111 us
    pallas_call x1, Pallas kernels: 130 us -> 109 us  [layer(): pl.pallas_call(functools.partial(layer_kernel, dp, tensor), name='layer',...]
where the time goes in v3:
time: 111 us
  Pallas kernels  111 us (100%)
    pallas_call x1, Pallas kernels, layer(): pl.pallas_call(functools.partial(layer_kernel, dp, tensor), name='layer',...  109 us

profile of v3, /device:TPU:1, one launch (start us, length us, event | category | flops | bytes accessed | tf_op | source)
XLA Modules:
  0.0 111.2 jit_solution(12133503957641048386)
XLA Ops:
  0.6 108.9 %layer.1 = (bf16[2,320,128]{2,1,0:T(8,128)(2,1)}, f32[24,8,128]{2,1,0:T(8,128)}) custom-call(bf16[3,160,256]{2,1,0:T(8,128)(2,1)} %w_ref.1, bf16[160,256]{1,0:T(8,128)(2,1)} %bitcast.17, bf16[320,128]{1,0:T(8,128)(2,1)} %bitcast.18, bf16[320,128]{1,0:T(8,128)(2,1)} %bitcast.19, bf16[2,2,5120]{2,1,0:T(2,128)(2,1)} %bitcast.20, f32[3,4,256]{2,1,0:T(4,128)} %conv_ref.1, ...), custom_call_target="tpu_custom_call" | custom-call | tf_op jit(solution)/shard_map/layer/pallas_call | solution.py:674
  109.5 1.7 %split.1 = (bf16[320,128]{1,0:T(8,128)(2,1)}, bf16[320,128]{1,0:T(8,128)(2,1)}, f32[2,2,5120]{2,1,0:T(2,128)}, f32[3,4,256]{2,1,0:T(4,128)}, f32[2]{0:T(128)}, /*index=5*/f32[2]{0:T(128)}, f32[1,128]{1,0:T(1,128)}) custom-call(bf16[2,320,128]{2,1,0:T(8,128)(2,1)} %get-tuple-element.16.res_ref, f32[24,8,128]{2,1,0:T(8,128)} %get-tuple-element.17.sum_ref), custom_call_target="tpu_custom_call" | custom-call | tf_op jit(solution)/shard_map/split/pallas_call | solution.py:742

commit v4 on v3

--- a/solution.py
+++ b/solution.py
@@ -175,7 +175,10 @@
             own = self.block(0, 0, h)
             self.along_y(own, 1, 1, 0, h)
             self.along_y(own, -1, 1, 0, h)
-            self.along_z(own, 0, h)
+
+    def own_to_z(self):
+        for h in range(2):
+            self.along_z(self.block(0, 0, h), 0, h)
 
     def own_to_core(self):
         for h in range(2):
@@ -302,9 +305,11 @@
 
     for copy in own:
         copy.wait()
+    early.own_to_z()
     late.start()
     early.start()
     set_out(0)
+    late.own_to_z()
     late.own_to_core()
     early.own_to_core()
     early.from_z(0)
@@ -322,6 +327,17 @@
         return 0
 
     lax.fori_loop(0, xt.shape[0] // 128, column, 0)
+
+    row = lax.broadcasted_iota(jnp.int32, (LEN, LEN), 0)
+    lane = lax.broadcasted_iota(jnp.int32, (LEN, LEN), 1)
+    wide_row = lax.broadcasted_iota(jnp.int32, (LEN, width), 0)
+    within, strict, xor = row >= lane, row > lane, row ^ lane
+    triangle = jnp.where(within, 1.0, 0.0).astype(BF16)
+    triangle_t = jnp.where(row <= lane, 1.0, 0.0).astype(BF16)
+    lane_1 = lax.broadcasted_iota(jnp.int32, (1, LEN), 1)
+    rate = sum(jnp.where(lane_1 == h, rate_ref[h], 0.0) for h in range(heads))
+    bias = sum(jnp.where(lane_1 == h, bias_ref[h], 0.0) for h in range(heads))
+    gain = gain_ref[...]
 
     def spread(a, steps):
         for s in steps:
@@ -346,6 +362,16 @@
             return 0
 
         lax.fori_loop(0, tensor, turn, 0)
+
+    def decays():
+        logits_t = dot(wg16[...], xt[...])
+        logits = jnp.concatenate([logits_t, jnp.zeros((LEN - 16, LEN), F32)], 0).T
+        pre = logits + bias
+        soft = jnp.maximum(pre, 0.0) + jnp.log1p(jnp.exp(-jnp.abs(pre)))
+        strength = 1.0 / (1.0 + jnp.exp(-logits))
+        cumulative = triangle_product(triangle, -rate * soft)
+        cumulative_t = cumulative.T
+        return logits, pre, soft, strength, cumulative, cumulative_t
 
     def contract(k):
         early.from_core(k)
@@ -374,7 +400,8 @@
         if deep:
             late.from_z(k - 1)
             landed(1, gr)
-            logits_t = dot(wg16[...], xt[...])
+            contract(k - 1)
+            logits, pre, soft, strength, cumulative, cumulative_t = decays()
         early.from_y(k)
         if not deep:
             late.from_z(k - 1)
@@ -390,29 +417,10 @@
     if far <= 2:
         landed(0, xr)
         landed(1, gr)
-        logits_t = dot(wg16[...], xt[...])
-        for j in range(far - 1):
+        logits, pre, soft, strength, cumulative, cumulative_t = decays()
+        for j in range(far):
             contract(j)
-    contract(far - 1)
     contract(far)
-
-    row = lax.broadcasted_iota(jnp.int32, (LEN, LEN), 0)
-    lane = lax.broadcasted_iota(jnp.int32, (LEN, LEN), 1)
-    wide_row = lax.broadcasted_iota(jnp.int32, (LEN, width), 0)
-    within, strict, xor = row >= lane, row > lane, row ^ lane
-    triangle = jnp.where(within, 1.0, 0.0).astype(BF16)
-    triangle_t = jnp.where(row <= lane, 1.0, 0.0).astype(BF16)
-    lane_1 = lax.broadcasted_iota(jnp.int32, (1, LEN), 1)
-    rate = sum(jnp.where(lane_1 == h, rate_ref[h], 0.0) for h in range(heads))
-    bias = sum(jnp.where(lane_1 == h, bias_ref[h], 0.0) for h in range(heads))
-    gain = gain_ref[...]
-
-    logits = jnp.concatenate([logits_t, jnp.zeros((LEN - 16, LEN), F32)], 0).T
-    pre = logits + bias
-    soft = jnp.maximum(pre, 0.0) + jnp.log1p(jnp.exp(-jnp.abs(pre)))
-    strength = 1.0 / (1.0 + jnp.exp(-logits))
-    cumulative = triangle_product(triangle, -rate * soft)
-    cumulative_t = cumulative.T
 
     before, gate, active = [], [], []
     for s in range(3):
@@ -467,25 +475,35 @@
             along_x(a, sz, t, h, h).start()
 
     def make(a, sz, build):
-        for sx in [2, *ways, 0] if opposite else [*ways, 0]:
-            t = owner(sz, sx)
-            parts[a, t] = build(pl.ds(pl.multiple_of(t * part, 16), part)).astype(BF16)
+        zh = (here.zh + sz) % nz
+        rows = pl.ds(pl.multiple_of(zh * nx * part, 16), nx * part)
+        parts[a, pl.ds(zh * nx, nx)] = build(rows).astype(BF16).reshape(nx, part, LEN)
+        if not isinstance(sz, int):
+            ship(a, sz)
+
+    def ship_across(a, sz):
+        for h in range(2):
+            across(a, sz, owner(sz, 2), h).start()
+
+    def ship_along(a, sz, side):
+        for h in range(2):
+            if not opposite or h != side:
+                along_x(a, sz, owner(sz, ways[side]), side, h).start()
 
     def ship(a, sz):
         if opposite:
-            for h in range(2):
-                across(a, sz, owner(sz, 2), h).start()
-        for side, way in enumerate(ways):
-            for h in range(2):
-                if not opposite or h != side:
-                    along_x(a, sz, owner(sz, way), side, h).start()
+            ship_across(a, sz)
+        for side in range(len(ways)):
+            ship_along(a, sz, side)
+
+    away = [2, 1, 3] if nz == 4 else [1]
 
     def each_away(body):
-        def step(sz, _):
-            body(sz)
+        def step(i, _):
+            body(jnp.where(i < 2, 2 - i, 3) if nz == 4 else i + 1)
             return 0
 
-        lax.fori_loop(1, nz, step, 0)
+        lax.fori_loop(0, nz - 1, step, 0)
 
     def second(a, steps):
         for sz in steps:
@@ -510,11 +528,7 @@
     def out_part(rows):
         return dot(wf[3, rows, :], core_low[...], NT)
 
-    def out_step(sz):
-        make(0, sz, out_part)
-        ship(0, sz)
-
-    each_away(out_step)
+    each_away(lambda sz: make(0, sz, out_part))
 
     def back_term(t, _):
         back[...] += dot(gr[t], wf[3, pl.ds(pl.multiple_of(t * part, 16), part), :])
@@ -580,11 +594,7 @@
             total = total + dot(wf[s, rows, :], low[:, s * width : (s + 1) * width], NT)
         return total
 
-    def grad_step(sz):
-        make(1, sz, grad_in)
-        ship(1, sz)
-
-    each_away(grad_step)
+    each_away(lambda sz: make(1, sz, grad_in))
     make(1, 0, grad_in)
 
     def gates(i, _):
@@ -603,7 +613,6 @@
         send(pack.at[pl.ds(there * each, each)], ry.at[here.y], rys.at[s - 1], ryr.at[s - 1], here.at_y(s))
     ry[here.y] = pack[pl.ds(here.y * each, each)]
 
-    away = range(1, nz)
     second(0, away)
     each_away(lambda sz: pass_on(1, sz))
     ship(1, 0)

time: 111 us -> 109 us (0.982)
  Pallas kernels: 111 us -> 108 us
    pallas_call x1, Pallas kernels: 109 us -> 107 us  [layer(): pl.pallas_call(functools.partial(layer_kernel, dp, tensor), name='layer',...]
where the time goes in v4:
time: 109 us
  Pallas kernels  108 us (99%)
    pallas_call x1, Pallas kernels, layer(): pl.pallas_call(functools.partial(layer_kernel, dp, tensor), name='layer',...  107 us

profile of v4, /device:TPU:1, one launch (start us, length us, event | category | flops | bytes accessed | tf_op | source)
XLA Modules:
  0.0 109.1 jit_solution(1409723095838605600)
XLA Ops:
  0.6 106.8 %layer.1 = (bf16[2,320,128]{2,1,0:T(8,128)(2,1)}, f32[24,8,128]{2,1,0:T(8,128)}) custom-call(bf16[3,160,256]{2,1,0:T(8,128)(2,1)} %w_ref.1, bf16[160,256]{1,0:T(8,128)(2,1)} %bitcast.17, bf16[320,128]{1,0:T(8,128)(2,1)} %bitcast.18, bf16[320,128]{1,0:T(8,128)(2,1)} %bitcast.19, bf16[2,2,5120]{2,1,0:T(2,128)(2,1)} %bitcast.20, f32[3,4,256]{2,1,0:T(4,128)} %conv_ref.1, ...), custom_call_target="tpu_custom_call" | custom-call | tf_op jit(solution)/shard_map/layer/pallas_call | solution.py:683
  107.4 1.7 %split.1 = (bf16[320,128]{1,0:T(8,128)(2,1)}, bf16[320,128]{1,0:T(8,128)(2,1)}, f32[2,2,5120]{2,1,0:T(2,128)}, f32[3,4,256]{2,1,0:T(4,128)}, f32[2]{0:T(128)}, /*index=5*/f32[2]{0:T(128)}, f32[1,128]{1,0:T(1,128)}) custom-call(bf16[2,320,128]{2,1,0:T(8,128)(2,1)} %get-tuple-element.16.res_ref, f32[24,8,128]{2,1,0:T(8,128)} %get-tuple-element.17.sum_ref), custom_call_target="tpu_custom_call" | custom-call | tf_op jit(solution)/shard_map/split/pallas_call | solution.py:751

commit v5 on v4

--- a/solution.py
+++ b/solution.py
@@ -535,8 +535,6 @@
         return 0
 
     lax.fori_loop(0, tensor, back_term, 0)
-    make(0, 0, out_part)
-    each_away(lambda sz: pass_on(0, sz))
 
     gain_grad = jnp.zeros((1, HEAD), F32)
     for h in range(heads):
@@ -560,6 +558,8 @@
         dc_all = jnp.where(lane == h, dc, dc_all)
         db_all = jnp.where(lane == heads + h, d_beta, db_all)
 
+    each_away(lambda sz: pass_on(0, sz))
+
     for s in range(1, nx):
         arrive(gx.at[back_of(s, nx, here.x)], gxs.at[s - 1], gxr.at[s - 1])
     gz[here.zh] = sum(gx[i] for i in range(nx))
@@ -596,6 +596,7 @@
 
     each_away(lambda sz: make(1, sz, grad_in))
     make(1, 0, grad_in)
+    make(0, 0, out_part)
 
     def gates(i, _):
         grad = dot(d_logits_t, xt[pl.ds(pl.multiple_of(i * 256, 256), 256), :], NT)

time: 109 us -> 107 us (0.982)
  Pallas kernels: 108 us -> 106 us
    pallas_call x1, Pallas kernels: 107 us -> 104 us  [layer(): pl.pallas_call(functools.partial(layer_kernel, dp, tensor), name='layer',...]
where the time goes in v5:
time: 107 us
  Pallas kernels  106 us (99%)
    pallas_call x1, Pallas kernels, layer(): pl.pallas_call(functools.partial(layer_kernel, dp, tensor), name='layer',...  104 us

profile of v5, /device:TPU:1, one launch (start us, length us, event | category | flops | bytes accessed | tf_op | source)
XLA Modules:
  0.0 106.7 jit_solution(9776978529265736964)
XLA Ops:
  0.6 104.3 %layer.1 = (bf16[2,320,128]{2,1,0:T(8,128)(2,1)}, f32[24,8,128]{2,1,0:T(8,128)}) custom-call(bf16[3,160,256]{2,1,0:T(8,128)(2,1)} %w_ref.1, bf16[160,256]{1,0:T(8,128)(2,1)} %bitcast.17, bf16[320,128]{1,0:T(8,128)(2,1)} %bitcast.18, bf16[320,128]{1,0:T(8,128)(2,1)} %bitcast.19, bf16[2,2,5120]{2,1,0:T(2,128)(2,1)} %bitcast.20, f32[3,4,256]{2,1,0:T(4,128)} %conv_ref.1, ...), custom_call_target="tpu_custom_call" | custom-call | tf_op jit(solution)/shard_map/layer/pallas_call | solution.py:684
  105.0 1.7 %split.1 = (bf16[320,128]{1,0:T(8,128)(2,1)}, bf16[320,128]{1,0:T(8,128)(2,1)}, f32[2,2,5120]{2,1,0:T(2,128)}, f32[3,4,256]{2,1,0:T(4,128)}, f32[2]{0:T(128)}, /*index=5*/f32[2]{0:T(128)}, f32[1,128]{1,0:T(1,128)}) custom-call(bf16[2,320,128]{2,1,0:T(8,128)(2,1)} %get-tuple-element.16.res_ref, f32[24,8,128]{2,1,0:T(8,128)} %get-tuple-element.17.sum_ref), custom_call_target="tpu_custom_call" | custom-call | tf_op jit(solution)/shard_map/split/pallas_call | solution.py:752
